TPU v7x, 32 devices: a whole 2x2x4 slice. The times are simulated.
32 devices in a mesh: seq: 4 (over y, core), shard: 8 (over z, x).
Axes of the slice: x: 2, y: 2, z: 4, core: 2. Of those that a mesh axis runs over, the one named last changes fastest.
Arguments:
- inputs: bfloat16 [16, 1184, 1024], P('shard', 'seq'), may hold values from -24 to 24
- cotangent: bfloat16 [16, 1184, 1024], P('shard', 'seq'), may hold values from -6 to 6
- first_gain: bfloat16 [1024], P('shard'), may hold values from 0.5 to 1.5
- first_shift: bfloat16 [1024], P('shard'), may hold values from -4 to 4
- joint_weight: bfloat16 [1024, 3072], P('shard'), may hold values from -0.203125 to 0.203125
- joint_bias: bfloat16 [2048], P('shard'), may hold values from -1.5 to 1.5
- output_weight: bfloat16 [1024, 1024], P('shard'), may hold values from -1.5 to 1.5
- output_bias: bfloat16 [1024], P('shard'), may hold values from -6 to 6
- second_gain: bfloat16 [1024], P('shard'), may hold values from 0.5 to 1.5
- second_shift: bfloat16 [1024], P('shard'), may hold values from -4 to 4
- expand_weight: bfloat16 [1024, 4096], P('shard'), may hold values from -0.203125 to 0.203125
- expand_bias: bfloat16 [4096], P('shard'), may hold values from -6 to 6
- reduce_weight: bfloat16 [4096, 1024], P('shard'), may hold values from -0.09375 to 0.09375
- reduce_bias: bfloat16 [1024], P('shard'), may hold values from -6 to 6
Outputs:
- layer_out: bfloat16 [16, 1184, 1024], P('shard', 'seq')
- input_grad: bfloat16 [16, 1184, 1024], P('shard', 'seq')
- first_gain_grad: float32 [1024], P(('seq', 'shard'))
- first_shift_grad: float32 [1024], P(('seq', 'shard'))
- joint_weight_grad: float32 [1024, 3072], P(('seq', 'shard'))
- joint_bias_grad: float32 [2048], P(('seq', 'shard'))
- output_weight_grad: float32 [1024, 1024], P(('seq', 'shard'))
- output_bias_grad: float32 [1024], P(('seq', 'shard'))
- second_gain_grad: float32 [1024], P(('seq', 'shard'))
- second_shift_grad: float32 [1024], P(('seq', 'shard'))
- expand_weight_grad: float32 [1024, 4096], P(('seq', 'shard'))
- expand_bias_grad: float32 [4096], P(('seq', 'shard'))
- reduce_weight_grad: float32 [4096, 1024], P(('seq', 'shard'))
- reduce_bias_grad: float32 [1024], P(('seq', 'shard'))
- root_means: float32 [3], replicated
All inputs are finite; a program needn't handle non-finite values.
Results may differ from a plain program's by a relative error of at most 0.009.
Values may be sent and summed in bfloat16 or wider, within the bound.
A program may use at most 256 MiB of HBM per device.

v0:
```python
import jax
import jax.numpy as jnp
from jax import lax
from jax.sharding import PartitionSpec as P

HEAD_DIM = 64
LEN = 592
VALID = 577
PACK = 2


def layer_norm(value, gain, shift):
    center = value - jnp.mean(value, axis=-1, keepdims=True)
    spread = jnp.mean(center * center, axis=-1, keepdims=True)
    return center * lax.rsqrt(spread + 1e-06) * gain + shift


def weight_grad(left, right):
    return lax.dot_general(
        left, right, (((0, 1), (0, 1)), ((), ())), preferred_element_type=jnp.float32
    )


def back_product(grad, matrix):
    return lax.dot_general(
        grad, matrix, (((2,), (1,)), ((), ())), preferred_element_type=jnp.float32
    )


def exact_gelu(value):
    return jax.nn.gelu(value, approximate=False)


def on_device(
    inputs,
    cotangent,
    first_gain,
    first_shift,
    joint_weight,
    joint_bias,
    output_weight,
    output_bias,
    second_gain,
    second_shift,
    expand_weight,
    expand_bias,
    reduce_weight,
    reduce_bias,
):
    images = inputs.shape[0]
    tokens = inputs.shape[1]
    full_seq = PACK * LEN
    pieces = images * PACK
    factor = HEAD_DIM ** (-0.5)
    begin = lax.axis_index("seq") * tokens
    local_places = begin + jnp.arange(tokens, dtype=jnp.int32)
    local_row = (local_places % LEN < VALID).astype(jnp.float32)
    local_mask = jnp.broadcast_to(local_row[None, :], (images, tokens))
    key_keep = jnp.arange(LEN, dtype=jnp.int32) < VALID
    weighting = local_mask[:, :, None]
    g1w, s1w, wj, bj, wo, bo, g2w, s2w, w1, b1, w2, b2 = (
        lax.all_gather(first_gain, "shard", axis=0, tiled=True),
        lax.all_gather(first_shift, "shard", axis=0, tiled=True),
        lax.all_gather(joint_weight, "shard", axis=0, tiled=True),
        lax.all_gather(joint_bias, "shard", axis=0, tiled=True),
        lax.all_gather(output_weight, "shard", axis=0, tiled=True),
        lax.all_gather(output_bias, "shard", axis=0, tiled=True),
        lax.all_gather(second_gain, "shard", axis=0, tiled=True),
        lax.all_gather(second_shift, "shard", axis=0, tiled=True),
        lax.all_gather(expand_weight, "shard", axis=0, tiled=True),
        lax.all_gather(expand_bias, "shard", axis=0, tiled=True),
        lax.all_gather(reduce_weight, "shard", axis=0, tiled=True),
        lax.all_gather(reduce_bias, "shard", axis=0, tiled=True),
    )
    g1f = g1w.astype(jnp.float32)
    s1f = s1w.astype(jnp.float32)
    bjf = bj.astype(jnp.float32)
    bof = bo.astype(jnp.float32)
    g2f = g2w.astype(jnp.float32)
    s2f = s2w.astype(jnp.float32)
    b1f = b1.astype(jnp.float32)
    b2f = b2.astype(jnp.float32)
    width = g1f.shape[0]
    xfull = inputs.astype(jnp.float32)
    normed1, first_back = jax.vjp(layer_norm, xfull, g1f, s1f)
    active1 = normed1.astype(jnp.bfloat16)
    bias_full = jnp.concatenate([bjf[:width], jnp.zeros((width,), jnp.float32), bjf[width:]])
    joint = (jnp.dot(active1, wj, preferred_element_type=jnp.float32) + bias_full).astype(
        jnp.bfloat16
    )
    joint = joint.reshape(images, tokens, 3, width)
    heads = lax.all_to_all(joint, "seq", split_axis=3, concat_axis=1, tiled=True)
    local_width = heads.shape[3]
    local_heads = local_width // HEAD_DIM
    query = heads[:, :, 0].reshape(pieces, LEN, local_heads, HEAD_DIM)
    keys = heads[:, :, 1].reshape(pieces, LEN, local_heads, HEAD_DIM)
    values = heads[:, :, 2].reshape(pieces, LEN, local_heads, HEAD_DIM)

    def score_block(qpart, kpart):
        raw = jnp.einsum("qhd,khd->hqk", qpart, kpart, preferred_element_type=jnp.float32) * factor
        return jnp.where(key_keep[None, None, :], raw, -1000000000.0)

    def attend(item):
        qpart, kpart, vpart = item
        scores = score_block(qpart, kpart)
        top = jnp.max(scores, axis=-1, keepdims=True)
        expo = jnp.exp(scores - top)
        total = jnp.sum(expo, axis=-1, keepdims=True)
        probs = expo / total
        logsum = (top + jnp.log(total))[:, :, 0]
        context = jnp.einsum(
            "hqk,khd->qhd", probs.astype(jnp.bfloat16), vpart, preferred_element_type=jnp.float32
        )
        return (context.astype(jnp.bfloat16).reshape(LEN, local_width), logsum)

    context, logsums = lax.map(attend, (query, keys, values))
    context = context.reshape(images, full_seq, local_width)
    gathered_ctx = lax.all_to_all(context, "seq", split_axis=1, concat_axis=2, tiled=True)
    attn = jnp.dot(gathered_ctx, wo, preferred_element_type=jnp.float32) + bof
    resid = xfull + attn
    normed2, second_back = jax.vjp(layer_norm, resid, g2f, s2f)
    active2 = normed2.astype(jnp.bfloat16)
    upper = jnp.dot(active2, w1, preferred_element_type=jnp.float32) + b1f
    activated, gelu_back = jax.vjp(exact_gelu, upper)
    hidden = activated.astype(jnp.bfloat16)
    branch = jnp.dot(hidden, w2, preferred_element_type=jnp.float32) + b2f
    result = resid + branch
    sums = jnp.stack(
        [
            jnp.sum(result * result * weighting),
            jnp.sum(attn * attn * weighting),
            jnp.sum(branch * branch * weighting),
        ]
    )
    counted = jnp.sum(local_mask) * width
    total_sums, total_count = lax.psum((sums, counted), ("seq", "shard"))
    root_means = jnp.sqrt(total_sums / total_count + 1e-06)
    wj, wo, w1, w2 = (
        lax.all_gather(joint_weight, "shard", axis=0, tiled=True),
        lax.all_gather(output_weight, "shard", axis=0, tiled=True),
        lax.all_gather(expand_weight, "shard", axis=0, tiled=True),
        lax.all_gather(reduce_weight, "shard", axis=0, tiled=True),
    )
    dout = cotangent.astype(jnp.float32) * weighting
    dout_low = dout.astype(jnp.bfloat16)
    grad_w2 = weight_grad(hidden, dout_low)
    grad_b2 = jnp.sum(dout, axis=(0, 1))
    dhidden = back_product(dout_low, w2)
    dupper = gelu_back(dhidden)[0].astype(jnp.bfloat16)
    grad_w1 = weight_grad(active2, dupper)
    grad_b1 = jnp.sum(dupper.astype(jnp.float32), axis=(0, 1))
    dactive2 = back_product(dupper, w1)
    dresid_norm, grad_g2, grad_s2 = second_back(dactive2)
    dresid = dout + dresid_norm
    dattn = dresid.astype(jnp.bfloat16)
    grad_wo = weight_grad(gathered_ctx, dattn)
    grad_bo = jnp.sum(dattn.astype(jnp.float32), axis=(0, 1))
    dcontext = back_product(dattn, wo).astype(jnp.bfloat16)
    dctx_heads = lax.all_to_all(dcontext, "seq", split_axis=2, concat_axis=1, tiled=True)
    dctx_heads = dctx_heads.reshape(pieces, LEN, local_heads, HEAD_DIM)

    def attend_back(item):
        qpart, kpart, vpart, logsum, dpart = item
        scores = score_block(qpart, kpart)
        probs = jnp.exp(scores - logsum[:, :, None])
        dprobs = jnp.einsum("qhd,khd->hqk", dpart, vpart, preferred_element_type=jnp.float32)
        dscore = (probs * (dprobs - jnp.sum(probs * dprobs, axis=-1, keepdims=True))).astype(
            jnp.bfloat16
        )
        dquery = (
            jnp.einsum("hqk,khd->qhd", dscore, kpart, preferred_element_type=jnp.float32) * factor
        )
        dkeys = (
            jnp.einsum("hqk,qhd->khd", dscore, qpart, preferred_element_type=jnp.float32) * factor
        )
        dvalues = jnp.einsum(
            "hqk,qhd->khd", probs.astype(jnp.bfloat16), dpart, preferred_element_type=jnp.float32
        )
        stacked = jnp.stack([dquery, dkeys, dvalues], axis=1).astype(jnp.bfloat16)
        return stacked.reshape(LEN, 3, local_width)

    dheads = lax.map(attend_back, (query, keys, values, logsums, dctx_heads))
    dheads = dheads.reshape(images, full_seq, 3, local_width)
    djoint = lax.all_to_all(dheads, "seq", split_axis=1, concat_axis=3, tiled=True)
    djoint = djoint.reshape(images, tokens, 3 * width)
    grad_wj = weight_grad(active1, djoint)
    joint_sums = jnp.sum(djoint.astype(jnp.float32), axis=(0, 1))
    grad_bj = jnp.concatenate([joint_sums[:width], joint_sums[2 * width :]])
    dactive1 = back_product(djoint, wj)
    dinput_norm, grad_g1, grad_s1 = first_back(dactive1)
    dinput = (dresid + dinput_norm).astype(jnp.bfloat16)
    (
        own_g1,
        own_s1,
        own_wj,
        own_bj,
        own_wo,
        own_bo,
        own_g2,
        own_s2,
        own_w1,
        own_b1,
        own_w2,
        own_b2,
    ) = (
        lax.psum_scatter(grad_g1, ("seq", "shard"), scatter_dimension=0, tiled=True),
        lax.psum_scatter(grad_s1, ("seq", "shard"), scatter_dimension=0, tiled=True),
        lax.psum_scatter(grad_wj, ("seq", "shard"), scatter_dimension=0, tiled=True),
        lax.psum_scatter(grad_bj, ("seq", "shard"), scatter_dimension=0, tiled=True),
        lax.psum_scatter(grad_wo, ("seq", "shard"), scatter_dimension=0, tiled=True),
        lax.psum_scatter(grad_bo, ("seq", "shard"), scatter_dimension=0, tiled=True),
        lax.psum_scatter(grad_g2, ("seq", "shard"), scatter_dimension=0, tiled=True),
        lax.psum_scatter(grad_s2, ("seq", "shard"), scatter_dimension=0, tiled=True),
        lax.psum_scatter(grad_w1, ("seq", "shard"), scatter_dimension=0, tiled=True),
        lax.psum_scatter(grad_b1, ("seq", "shard"), scatter_dimension=0, tiled=True),
        lax.psum_scatter(grad_w2, ("seq", "shard"), scatter_dimension=0, tiled=True),
        lax.psum_scatter(grad_b2, ("seq", "shard"), scatter_dimension=0, tiled=True),
    )
    return (
        result.astype(jnp.bfloat16),
        dinput,
        own_g1,
        own_s1,
        own_wj,
        own_bj,
        own_wo,
        own_bo,
        own_g2,
        own_s2,
        own_w1,
        own_b1,
        own_w2,
        own_b2,
        root_means,
    )


def solution(mesh):
    return jax.shard_map(
        on_device,
        mesh=mesh,
        in_specs=(
            P("shard", "seq", None),
            P("shard", "seq", None),
            P("shard"),
            P("shard"),
            P("shard", None),
            P("shard"),
            P("shard", None),
            P("shard"),
            P("shard"),
            P("shard"),
            P("shard", None),
            P("shard"),
            P("shard", None),
            P("shard"),
        ),
        out_specs=(
            P("shard", "seq", None),
            P("shard", "seq", None),
            P(("seq", "shard")),
            P(("seq", "shard")),
            P(("seq", "shard"), None),
            P(("seq", "shard")),
            P(("seq", "shard"), None),
            P(("seq", "shard")),
            P(("seq", "shard")),
            P(("seq", "shard")),
            P(("seq", "shard"), None),
            P(("seq", "shard")),
            P(("seq", "shard"), None),
            P(("seq", "shard")),
            P(),
        ),
        check_vma=False,
    )
```

profile of v0, /device:TPU:0, one launch (start us, length us, event | category | flops | bytes accessed | tf_op | source)
XLA Modules:
  0.0 1544.2 jit_solution(372224842233786760)
XLA Ops:
  9.4 22.5 %all-gather = bf16[8,1,128]{2,1,0:T(2,128)(2,1)S(1)} all-gather(bf16[1,1,128]{2,1,0:T(2,128)(2,1)} %bitcast.236), channel_id=1, replica_groups=mesh['seq'=4,'shard'=8] {'shard'}, dimensions={0}, use_global_device_ids=true | all-gather | bytes 2304 | tf_op jit(solution)/shard_map/all_gather | solution.py:62
  32.6 16.6 %all-gather.1 = bf16[8,1,128]{2,1,0:T(2,128)(2,1)S(1)} all-gather(bf16[1,1,128]{2,1,0:T(2,128)(2,1)} %bitcast.237), channel_id=1, replica_groups=mesh['seq'=4,'shard'=8] {'shard'}, dimensions={0}, use_global_device_ids=true | all-gather | bytes 2304 | tf_op jit(solution)/shard_map/all_gather | solution.py:63
  49.2 18.5 %all-gather.2 = bf16[8,1,256]{2,1,0:T(2,128)(2,1)S(1)} all-gather(bf16[1,1,256]{2,1,0:T(2,128)(2,1)S(1)} %reshape.219), channel_id=1, replica_groups=mesh['seq'=4,'shard'=8] {'shard'}, dimensions={0}, use_global_device_ids=true | all-gather | bytes 4608 | tf_op jit(solution)/shard_map/all_gather | solution.py:65
  69.8 42.3 %all-gather.13.cloned.1.call-done = bf16[1024,3072]{1,0:T(8,128)(2,1)} async-done(((bf16[128,3072]{1,0:T(8,128)(2,1)}), bf16[1024,3072]{1,0:T(8,128)(2,1)}) %all-gather.13.cloned.1.call-update) | async-done | bytes 6291472 | tf_op jit(solution)/shard_map/all_gather | solution.py:64
  112.1 8.5 add_convert_fusion.1
  120.6 11.5 reshape.210
  132.1 16.5 %copy.86 = bf16[2,296,3,1024]{1,0,2,3:T(2,128)(2,1)} copy(bf16[2,296,3,1024]{3,2,1,0:T(4,128)(2,1)} %reshape.210) | data formatting | bytes 7274496 | tf_op jit(solution)/shard_map/reshape | solution.py:91
  148.6 4.9 all-to-all-start
  154.2 53.2 %all-to-all-done = bf16[2,296,3,1024]{1,0,2,3:T(2,128)(2,1)} async-done(((bf16[2,296,3,1024]{1,0,2,3:T(2,128)(2,1)}), bf16[2,296,3,1024]{1,0,2,3:T(2,128)(2,1)}, u32[]{:S(2)}, u32[]{:S(2)}) %all-to-all-start) | async-done | bytes 3637280 | tf_op jit(solution)/shard_map/all_to_all | solution.py:92
  207.4 13.1 copy.113
  220.5 2.5 copy.88
  224.7 4.6 reshape.249
  229.3 4.2 copy.92
  235.5 3.2 copy.93
  238.7 4.6 reshape.251
  243.3 4.2 copy.94
  247.6 29.7 %while.24 = (s32[]{:T(128)}, bf16[4,592,256]{2,1,0:T(8,128)(2,1)}, f32[4,4,592]{2,1,0:T(4,128)S(1)}, bf16[4,592,4,64]{1,3,2,0:T(8,128)(2,1)}, bf16[4,592,4,64]{1...) while((s32[]{:T(128)}, bf16[4,592,256]{2,1,0:T(8,128)(2,1)}, ...), condition=%wide.region_5.6_spmd.clone, body=%wide.region_2.5_spmd.clone.sunk | while | flops 375847168 | bytes 19403840 | solution.py:116
  251.4 2.7 fusion.147
  258.8 2.7 fusion.147
  262.5 2.4 fusion.145
  266.3 2.7 fusion.147
  273.7 2.7 fusion.147
  277.4 9.3 copy.96
  286.6 4.3 all-to-all-start.1
  290.9 17.7 %all-gather.3 = bf16[8,1,128]{2,1,0:T(2,128)(2,1)S(1)} all-gather(bf16[1,1,128]{2,1,0:T(2,128)(2,1)S(1)} %bitcast.238), channel_id=1, replica_groups=mesh['seq'=4,'shard'=8] {'shard'}, dimensions={0}, use_global_device_ids=true | all-gather | bytes 2304 | tf_op jit(solution)/shard_map/all_gather | solution.py:67
  308.6 17.1 %all-gather.4 = bf16[8,1,128]{2,1,0:T(2,128)(2,1)S(1)} all-gather(bf16[1,1,128]{2,1,0:T(2,128)(2,1)S(1)} %bitcast.239), channel_id=1, replica_groups=mesh['seq'=4,'shard'=8] {'shard'}, dimensions={0}, use_global_device_ids=true | all-gather | bytes 2304 | tf_op jit(solution)/shard_map/all_gather | solution.py:68
  325.7 26.3 %all-gather.6 = bf16[8,1,512]{2,1,0:T(2,128)(2,1)S(1)} all-gather(bf16[1,1,512]{2,1,0:T(2,128)(2,1)S(1)} %reshape.227), channel_id=1, replica_groups=mesh['seq'=4,'shard'=8] {'shard'}, dimensions={0}, use_global_device_ids=true | all-gather | bytes 9216 | tf_op jit(solution)/shard_map/all_gather | solution.py:71
  352.1 16.5 %all-gather.5 = bf16[8,1,128]{2,1,0:T(2,128)(2,1)S(1)} all-gather(bf16[1,1,128]{2,1,0:T(2,128)(2,1)S(1)} %bitcast.240), channel_id=1, replica_groups=mesh['seq'=4,'shard'=8] {'shard'}, dimensions={0}, use_global_device_ids=true | all-gather | bytes 2304 | tf_op jit(solution)/shard_map/all_gather | solution.py:69
  368.6 18.3 %all-gather.7 = bf16[8,1,128]{2,1,0:T(2,128)(2,1)S(1)} all-gather(bf16[1,1,128]{2,1,0:T(2,128)(2,1)S(1)} %bitcast.241), channel_id=1, replica_groups=mesh['seq'=4,'shard'=8] {'shard'}, dimensions={0}, use_global_device_ids=true | all-gather | bytes 2304 | tf_op jit(solution)/shard_map/all_gather | solution.py:73
  389.7 4.9 fusion.113
  396.4 16.1 %fusion.87 = (u8[296,4096]{1,0:T(8,128)(4,1)S(1)}, u8[296,4096]{1,0:T(8,128)(4,1)S(1)}, f32[2,296,4096]{2,1,0:T(8,128)}) fusion(f32[4096]{0:T(1024)S(1)} %bitcast.219, bf16[1024,4096]{1,0:T(8,128)(2,1)} %all-gather.17.cloned.1.call-done, f32[2,296,1024]{2,1,0:T(8,128)} %copy-done.1, f32[1024]{0:T(1024)S(1)} %bitcast.217, f32[1024]{0:T(1024)S(1)} %bitcast.213, ...), kind=kOutput, calls=%fused_computation.130 | convolution fusion | flops 5000609792 | bytes 22966912 | tf_op jit(solution)/shard_map/dot_general | solution.py:123
  412.5 25.3 %multiply_convert_fusion.1 = (bf16[2,296,4096]{2,1,0:T(8,128)(2,1)}, f32[2,296,4096]{2,1,0:T(8,128)}) fusion(f32[2,296,4096]{2,1,0:T(8,128)} %get-tuple-element.239, f32[4096]{0:T(1024)S(1)} %bitcast.220, u8[296,4096]{1,0:T(8,128)(4,1)S(1)} %get-tuple-element.168, u8[296,4096]{1,0:T(8,128)(4,1)S(1)} %get-tuple-element.167), kind=kLoop, calls=%fused_computation.70 | loop fusion | flops 172163072 | bytes 26689536 | tf_op jit(solution)/shard_map/convert_element_type | solution.py:125
  437.8 17.3 %convert_reduce_fusion = (f32[4096]{0:T(1024)}, bf16[2,296,4096]{2,1,0:T(8,128)(2,1)}) fusion(f32[2,296,4096]{2,1,0:T(8,128)} %get-tuple-element.223, bf16[4096,1024]{1,0:T(8,128)(2,1)} %all-gather.19.cloned.1.call-done, bf16[2,296,1024]{2,1,0:T(8,128)(2,1)S(1)} %copy-done.12, f32[296]{0:T(512)S(1)} %fusion.105, f32[2,296,4096]{2,1,0:T(8,128)} %get-tuple-element.239, ...), kind=kOutput, calls=%fused_computation.68 | convolution fusion | flops 5009092608 | bytes 33883296 | tf_op jit(solution)/shard_map/dot_general | solution.py:25
  455.1 9.4 fusion.61
  465.1 8.7 multiply_reduce_fusion.3
  479.8 3.0 copy.99
  482.8 3.6 all-to-all-start.2
  486.5 5.5 convolution_bitcast_fusion.3
  492.0 15.8 %all-to-all-done.2 = bf16[2,296,1024]{1,0,2:T(2,128)(2,1)S(1)} async-done(((bf16[2,296,1024]{1,0,2:T(2,128)(2,1)}), bf16[2,296,1024]{1,0,2:T(2,128)(2,1)S(1)}, u32[]{:S(2)}, u32[]{:S(2)}) %all-to-all-start.2) | async-done | bytes 1212448 | tf_op jit(solution)/shard_map/all_to_all | solution.py:159
  507.9 3.2 copy.128
  511.0 3.9 reshape.212
  516.2 56.1 %while.25 = (s32[]{:T(128)}, bf16[4,592,3,256]{3,1,0,2:T(8,128)(2,1)}, bf16[4,592,4,64]{1,3,2,0:T(8,128)(2,1)}, bf16[4,592,4,64]{1,3,2,0:T(8,128)(2,1)S(1)}, f32...) while((s32[]{:T(128)}, ...), condition=%wide.region_12.13_spmd.clone, body=%wide.region_10.12_spmd.clone.sunk | while | flops 919880960 | bytes 51014300 | solution.py:182
  518.2 3.1 multiply_reduce_fusion.8
  525.8 2.5 fusion.157
  532.2 3.1 multiply_reduce_fusion.8
  539.9 2.5 fusion.157
  546.3 3.1 multiply_reduce_fusion.8
  553.9 2.5 fusion.157
  560.3 3.1 multiply_reduce_fusion.8
  568.0 2.5 fusion.157
  572.3 16.9 %copy.106 = bf16[2,1184,3,256]{3,0,2,1:T(2,128)(2,1)S(1)} copy(bf16[2,1184,3,256]{3,1,0,2:T(8,128)(2,1)} %bitcast.209) | data formatting | bytes 7274496 | tf_op jit(solution)/shard_map/reshape | solution.py:183
  589.2 51.4 %all_to_all.66 = bf16[2,1184,3,256]{3,0,2,1:T(2,128)(2,1)S(1)} all-to-all(bf16[2,1184,3,256]{3,0,2,1:T(2,128)(2,1)S(1)} %copy.106), channel_id=1, replica_groups=mesh['seq'=4,'shard'=8] {'seq'}, dimensions={1} | all-to-all | bytes 7274496 | tf_op jit(solution)/shard_map/all_to_all | solution.py:184
  643.1 3.2 copy.108
  646.3 7.6 reshape.214
  653.9 10.2 convolution_bitcast_fusion.2
  665.9 13.1 convolution_bitcast_fusion.1
  680.3 13.3 convolution_bitcast_fusion
  696.9 2.7 convert_reduce_fusion.1
  699.7 8.0 fusion.109
  709.1 41.2 %all-reduce.8 = (f32[1024]{0:T(1024)S(1)}, f32[1024]{0:T(1024)S(1)}, f32[2048]{0:T(1024)S(1)}, f32[1024]{0:T(1024)S(1)}, f32[1024]{0:T(1024)S(1)}, /*index=5*/f3...) all-reduce(f32[1024]{0:T(1024)S(1)} %get-tuple-element.171, ...), channel_id=2, replica_groups=mesh['seq'=4,'shard'=8] {'seq','shard'}, use_global_device_ids=true, to_apply=%region_16.17.clone | all-reduce | flops 12292 | bytes 98336
  756.2 3.8 add_convert_fusion.2
  760.0 56.6 %reduce-scatter.5.cloned.1.call-done = f32[32,3072]{1,0:T(8,128)} async-done(((f32[1024,3072]{1,0:T(8,128)}), f32[32,3072]{1,0:T(8,128)}) %reduce-scatter.5.cloned.1.call-update) | async-done | bytes 393232 | tf_op jit(solution)/shard_map/reduce_scatter | solution.py:208
  816.7 360.2 %reduce-scatter.9.cloned.1.call-done = f32[32,4096]{1,0:T(8,128)} async-done(((f32[1024,4096]{1,0:T(8,128)}), f32[32,4096]{1,0:T(8,128)}) %reduce-scatter.9.cloned.1.call-update) | async-done | bytes 524304 | tf_op jit(solution)/shard_map/reduce_scatter | solution.py:214
  1176.8 360.3 %reduce-scatter.11.cloned.1.call-done = f32[128,1024]{1,0:T(8,128)} async-done(((f32[4096,1024]{1,0:T(8,128)}), f32[128,1024]{1,0:T(8,128)}) %reduce-scatter.11.cloned.1.call-update) | async-done | bytes 524304 | tf_op jit(solution)/shard_map/reduce_scatter | solution.py:216
  (216 shorter events, 86.8 us)
Async XLA Ops:
  7.2 62.1 %copy-start.6 = (bf16[2,296,1024]{2,1,0:T(8,128)(2,1)S(1)}, bf16[2,296,1024]{2,1,0:T(8,128)(2,1)}, u32[]{:S(2)}) copy-start(bf16[2,296,1024]{2,1,0:T(8,128)(2,1)} %param.18) | copy-start | bytes 3637252
  7.2 104.9 %all-gather.13.cloned.1.call-start = ((), (), s32[]{:S(2)}) async-start(), calls=%async_computation.8 | async-start | bytes 7077888 | tf_op jit(solution)/shard_map/all_gather | solution.py:64
  7.9 381.7 %all-gather.15.cloned.1.call-start = ((), (), s32[]{:S(2)}) async-start(), calls=%async_computation.9 | async-start | bytes 2359296 | tf_op jit(solution)/shard_map/all_gather | solution.py:66
  8.7 387.7 %all-gather.17.cloned.1.call-start = ((), (), s32[]{:S(2)}) async-start(), calls=%async_computation.10 | async-start | bytes 9437184 | tf_op jit(solution)/shard_map/all_gather | solution.py:70
  31.9 88.7 %copy-start.19 = (f32[8,1,128]{2,1,0:T(1,128)}, f32[8,1,128]{2,1,0:T(1,128)S(1)}, u32[]{:S(2)}) copy-start(f32[8,1,128]{2,1,0:T(1,128)S(1)} %convert_element_type.124) | copy-start | bytes 12292
  49.2 71.4 %copy-start.32 = (f32[8,1,128]{2,1,0:T(1,128)}, f32[8,1,128]{2,1,0:T(1,128)S(1)}, u32[]{:S(2)}) copy-start(f32[8,1,128]{2,1,0:T(1,128)S(1)} %convert_element_type.125) | copy-start | bytes 12292
  69.3 51.3 %copy-start.17 = (f32[2,296]{1,0:T(2,128)}, f32[2,296]{1,0:T(2,128)S(1)}, u32[]{:S(2)}) copy-start(f32[2,296]{1,0:T(2,128)S(1)} %broadcast_multiply_fusion.1) | copy-start | bytes 7108
  69.7 50.8 %copy-start.23 = (f32[2,296]{1,0:T(2,128)}, f32[2,296]{1,0:T(2,128)S(1)}, u32[]{:S(2)}) copy-start(f32[2,296]{1,0:T(2,128)S(1)} %fusion.82) | copy-start | bytes 7108
  69.8 50.8 %copy-start.21 = (f32[2,296]{1,0:T(2,128)}, f32[2,296]{1,0:T(2,128)S(1)}, u32[]{:S(2)}) copy-start(f32[2,296]{1,0:T(2,128)S(1)} %fusion.107) | copy-start | bytes 7108
  148.6 58.8 %all-to-all-start = ((bf16[2,296,3,1024]{1,0,2,3:T(2,128)(2,1)}), bf16[2,296,3,1024]{1,0,2,3:T(2,128)(2,1)}, u32[]{:S(2)}, u32[]{:S(2)}) async-start(bf16[2,296,3,1024]{1,0,2,3:T(2,128)(2,1)} %copy.86), calls=%async_computation | async-start | bytes 9437184 | tf_op jit(solution)/shard_map/all_to_all | solution.py:92
  153.6 284.2 %all-gather.19.cloned.1.call-start = ((), (), s32[]{:S(2)}) async-start(), calls=%async_computation.11 | async-start | bytes 9437184 | tf_op jit(solution)/shard_map/all_gather | solution.py:72
  277.3 13.6 copy-start.35
  277.3 31.3 %copy-start.36 = (bf16[128]{0:T(256)(128)(2,1)S(1)}, bf16[128]{0:T(256)(128)(2,1)}, u32[]{:S(2)}) copy-start(bf16[128]{0:T(256)(128)(2,1)} %param.26) | copy-start | bytes 772
  277.3 48.4 %copy-start.34 = (bf16[512]{0:T(512)(128)(2,1)S(1)}, bf16[512]{0:T(512)(128)(2,1)}, u32[]{:S(2)}) copy-start(bf16[512]{0:T(512)(128)(2,1)} %param.29) | copy-start | bytes 3076
  277.3 74.7 %copy-start.37 = (bf16[128]{0:T(256)(128)(2,1)S(1)}, bf16[128]{0:T(256)(128)(2,1)}, u32[]{:S(2)}) copy-start(bf16[128]{0:T(256)(128)(2,1)} %param.27) | copy-start | bytes 772
  277.3 91.2 %copy-start.38 = (bf16[128]{0:T(256)(128)(2,1)S(1)}, bf16[128]{0:T(256)(128)(2,1)}, u32[]{:S(2)}) copy-start(bf16[128]{0:T(256)(128)(2,1)} %param.31) | copy-start | bytes 772
  286.6 100.3 %all-to-all-start.1 = ((bf16[2,1184,256]{2,0,1:T(2,128)(2,1)}), bf16[2,1184,256]{2,0,1:T(2,128)(2,1)}, u32[]{:S(2)}, u32[]{:S(2)}) async-start(bf16[2,1184,256]{2,0,1:T(2,128)(2,1)} %copy.96), calls=%async_computation.1 | async-start | bytes 2424832 | tf_op jit(solution)/shard_map/all_to_all | solution.py:118
  368.5 27.9 %copy-start.15 = (f32[8,1,128]{2,1,0:T(1,128)}, f32[8,1,128]{2,1,0:T(1,128)S(1)}, u32[]{:S(2)}) copy-start(f32[8,1,128]{2,1,0:T(1,128)S(1)} %convert_element_type.129) | copy-start | bytes 12292
  394.6 1.4 copy-start.1
  412.5 25.3 %copy-start.12 = (bf16[2,296,1024]{2,1,0:T(8,128)(2,1)S(1)}, bf16[2,296,1024]{2,1,0:T(8,128)(2,1)}, u32[]{:S(2)}) copy-start(bf16[2,296,1024]{2,1,0:T(8,128)(2,1)} %param.19) | copy-start | bytes 3637252
  455.1 9.4 copy-start.2
  455.1 9.4 copy-start.11
  455.1 9.4 copy-start.39
  455.1 10.0 copy-start.41
  474.7 1.5 copy-start.4
  474.7 3.6 copy-start.40
  474.7 5.1 copy-start.25
  477.2 1.0 copy-start.14
  482.8 25.0 %all-to-all-start.2 = ((bf16[2,296,1024]{1,0,2:T(2,128)(2,1)}), bf16[2,296,1024]{1,0,2:T(2,128)(2,1)S(1)}, u32[]{:S(2)}, u32[]{:S(2)}) async-start(bf16[2,296,1024]{1,0,2:T(2,128)(2,1)} %copy.99), calls=%async_computation.2 | async-start | bytes 3145728 | tf_op jit(solution)/shard_map/all_to_all | solution.py:159
  486.4 273.6 %reduce-scatter.7.cloned.1.call-start = ((), (), s32[]{:S(2)}) async-start(), calls=%async_computation.13 | async-start | bytes 4325376 | tf_op jit(solution)/shard_map/reduce_scatter | solution.py:210
  492.0 324.7 %reduce-scatter.5.cloned.1.call-start = ((), (), s32[]{:S(2)}) async-start(), calls=%async_computation.12 | async-start | bytes 12976128 | tf_op jit(solution)/shard_map/reduce_scatter | solution.py:208
  641.2 1.9 copy-start
  646.2 7.6 copy-start.7
  646.2 7.6 copy-start.18
  646.3 7.7 copy-start.20
  646.3 7.7 copy-start.22
  646.3 7.7 copy-start.33
  664.2 1.7 copy-start.3
  664.2 1.7 copy-start.16
  664.2 512.6 %reduce-scatter.9.cloned.1.call-start = ((), (), s32[]{:S(2)}) async-start(), calls=%async_computation.14 | async-start | bytes 17301504 | tf_op jit(solution)/shard_map/reduce_scatter | solution.py:214
  678.9 1.3 copy-start.13
  679.0 858.2 %reduce-scatter.11.cloned.1.call-start = ((), (), s32[]{:S(2)}) async-start(), calls=%async_computation.15 | async-start | bytes 17301504 | tf_op jit(solution)/shard_map/reduce_scatter | solution.py:216
  693.6 6.1 copy-start.8
  699.7 8.1 copy-start.24
  699.7 8.1 copy-start.9
  707.7 1.5 copy-start.10
  707.7 1.5 copy-start.27
  707.7 1.5 copy-start.28
  707.7 1.4 copy-start.29
  707.7 1.4 copy-start.30
  707.7 1.4 copy-start.31
  707.7 48.5 %copy-start.5 = (f32[2,296,1024]{2,1,0:T(8,128)S(1)}, f32[2,296,1024]{2,1,0:T(8,128)}, u32[]{:S(2)}) copy-start(f32[2,296,1024]{2,1,0:T(8,128)} %copy-done.4) | copy-start | bytes 7274500
  707.7 48.5 %copy-start.26 = (f32[2,296]{1,0:T(2,128)S(1)}, f32[2,296]{1,0:T(2,128)}, u32[]{:S(2)}) copy-start(f32[2,296]{1,0:T(2,128)} %copy-done.25) | copy-start | bytes 7108
Sparse Core Ops, SparseCore 0:
  10.2 101.8 all-gather.12
  114.2 47.4 all-gather.14
  163.8 123.4 all-gather.16
  289.3 123.5 all-gather.18
  492.1 141.5 reduce-scatter.6
  664.3 152.2 reduce-scatter.4
  819.6 357.1 reduce-scatter.8
  1179.8 357.3 reduce-scatter.10
where the time goes:
time: 1550 us; the launch traced here: 1540 us
  waiting for transfers between devices  891 us (57%)
  blocking collectives  246 us (16%)
  matrix products  178 us (11%)
  local copies, waits for them, and re-layouts  145 us (9%)
  other arithmetic  55.2 us (4%)
  between operations  15.6 us (1%)
    reduce_scatter x1, waiting for transfers between devices, on_device(): lax.psum_scatter(grad_w2, ('seq', 'shard'), scatter_dimension=0, tiled=True)  360 us
    reduce_scatter x1, waiting for transfers between devices, on_device(): lax.psum_scatter(grad_w1, ('seq', 'shard'), scatter_dimension=0, tiled=True)  360 us
    reduce_scatter x1, waiting for transfers between devices, on_device(): lax.psum_scatter(grad_wj, ('seq', 'shard'), scatter_dimension=0, tiled=True)  56.6 us
    all_to_all x1, waiting for transfers between devices, on_device(): lax.all_to_all(joint, 'seq', split_axis=3, concat_axis=1, tiled=True)  53.2 us
    all_to_all x1, blocking collectives, on_device(): lax.all_to_all(dheads, 'seq', split_axis=1, concat_axis=3, tiled=True)  51.4 us
    all_gather x1, waiting for transfers between devices, on_device(): lax.all_gather(joint_weight, 'shard', axis=0, tiled=True)  42.3 us
    dot_general x4, matrix products, weight_grad(): lax.dot_general(left, right, (((0, 1), (0, 1)), ((), ())), preferred_elem...  42.1 us
    unnamed x1, blocking collectives  41.2 us
  transfers between devices with their start and end apart: 11, of which 6 were waited for; matrix products, arithmetic and copies ran while one was open for 21% of the time, Pallas kernels for 0%

commit v1 on v0

--- a/solution.py
+++ b/solution.py
@@ -1,12 +1,23 @@
+import functools
+
 import jax
 import jax.numpy as jnp
 from jax import lax
+from jax.experimental import pallas as pl
+from jax.experimental.pallas import tpu as pltpu
 from jax.sharding import PartitionSpec as P
 
+MESH = pl.DeviceIdType.MESH
+F32 = jnp.float32
+LOW = jnp.bfloat16
 HEAD_DIM = 64
 LEN = 592
 VALID = 577
 PACK = 2
+CUT = VALID // 16 * 16
+SLOTS = 8
+LEAD = (0, 2, 3, 4, 6)
+VMEM_LIMIT = 58 << 20
 
 
 def layer_norm(value, gain, shift):
@@ -235,9 +246,689 @@
     )
 
 
+def place():
+    seq = lax.axis_index("seq")
+    shard = lax.axis_index("shard")
+    return lax.rem(shard, 2), lax.div(seq, 2), lax.div(shard, 2), lax.rem(seq, 2)
+
+
+def z_partner(z, k):
+    if k == 0:
+        return z
+    if k == 1:
+        return z + 1 - 2 * lax.rem(z, 2)
+    if k == 2:
+        return lax.rem(z + 2, 4)
+    return 3 - z
+
+
+def dev(x, y, z, c):
+    return (y * 2 + c, z * 2 + x)
+
+
+def remote(src, dst, sem, target):
+    return pltpu.make_async_remote_copy(
+        src_ref=src,
+        dst_ref=dst,
+        send_sem=sem.at[0],
+        recv_sem=sem.at[1],
+        device_id=target,
+        device_id_type=MESH,
+    )
+
+
+def greet():
+    x, y, z, c = place()
+    barrier = pltpu.get_barrier_semaphore()
+    near = [dev(x, y, z_partner(z, k), c) for k in (1, 2, 3)]
+    near += [dev(1 - x, y, z, c), dev(x, 1 - y, z, c), dev(x, y, z, 1 - c)]
+    for who in near:
+        pl.semaphore_signal(barrier, inc=1, device_id=who, device_id_type=MESH)
+    pl.semaphore_wait(barrier, len(near))
+
+
+class Gather:
+    def __init__(self, part, full, piece, sems, slot):
+        self.part, self.full = part, full
+        self.zs, self.xs, self.ys, self.cs, self.es, self.own = [s.at[slot] for s in sems]
+        self.shard_rows = part.shape[0]
+        self.row, self.rows, self.col, self.cols = piece
+        edge = self.cols * 3 // 8 // 128 * 128
+        span = self.cols - edge
+        self.x, self.y, self.z, self.c = place()
+        self.duty = pl.ds(pl.multiple_of(self.col + self.y * edge, 128), span)
+        self.mine = pl.ds(pl.multiple_of(self.col + self.y * span, 128), edge)
+        self.other = pl.ds(pl.multiple_of(self.col + (1 - self.y) * span, 128), edge)
+
+    def half(self, k, j):
+        x = self.x if j == 0 else 1 - self.x
+        shard = z_partner(self.z, k) * 2 + x
+        half = self.rows // 2
+        first = shard * self.shard_rows + self.row + self.c * half
+        return pl.ds(pl.multiple_of(first, 16), half)
+
+    def copy(self, k, j, cols, sem, target, local=False):
+        at = (self.half(k, j), cols)
+        src = self.full.at[at]
+        if local:
+            half = self.rows // 2
+            src = self.part.at[pl.ds(pl.multiple_of(self.row + self.c * half, 16), half), cols]
+        return remote(src, self.full.at[at], sem, target)
+
+    def over_z(self, k):
+        target = dev(self.x, self.y, z_partner(self.z, k), self.c)
+        return self.copy(0, 0, self.duty, self.zs.at[k - 1], target, local=True)
+
+    def over_x(self, k):
+        target = dev(1 - self.x, self.y, self.z, self.c)
+        return self.copy(k, 0, self.duty, self.xs.at[k], target, local=k == 0)
+
+    def over_y(self, k, j):
+        target = dev(self.x, 1 - self.y, self.z, self.c)
+        return self.copy(k, j, self.mine, self.ys.at[k * 2 + j], target)
+
+    def over_core(self, k, j):
+        target = dev(self.x, self.y, self.z, 1 - self.c)
+        return self.copy(k, j, self.duty, self.cs.at[k * 2 + j], target)
+
+    def over_core_rest(self, k, j):
+        target = dev(self.x, self.y, self.z, 1 - self.c)
+        return self.copy(k, j, self.other, self.es.at[k * 2 + j], target)
+
+    def own_copy(self):
+        shard = self.z * 2 + self.x
+        cols = pl.ds(self.col, self.cols)
+        rows = pl.ds(pl.multiple_of(shard * self.shard_rows + self.row, 16), self.rows)
+        src = self.part.at[pl.ds(self.row, self.rows), cols]
+        return pltpu.make_async_copy(src, self.full.at[rows, cols], self.own.at[0])
+
+    def step0(self):
+        for k in (1, 2, 3):
+            self.over_z(k).start()
+        self.over_x(0).start()
+        self.own_copy().start()
+
+    def step1(self):
+        for k in (1, 2, 3):
+            self.over_z(k).wait_recv()
+            self.over_x(k).start()
+            self.over_y(k, 0).start()
+            self.over_core(k, 0).start()
+
+    def step2(self):
+        for k in (0, 1, 2, 3):
+            self.over_x(k).wait_recv()
+            self.over_y(k, 1).start()
+            self.over_core(k, 1).start()
+
+    def others(self):
+        return [(k, 0) for k in (1, 2, 3)] + [(k, 1) for k in (0, 1, 2, 3)]
+
+    def step3(self):
+        for k, j in self.others():
+            self.over_y(k, j).wait_recv()
+            self.over_core_rest(k, j).start()
+
+    def step4(self):
+        for k, j in self.others():
+            self.over_core(k, j).wait()
+            self.over_core_rest(k, j).wait()
+            self.over_y(k, j).wait_send()
+        for k in (1, 2, 3):
+            self.over_z(k).wait_send()
+        for k in range(4):
+            self.over_x(k).wait_send()
+        self.own_copy().wait()
+
+
+class SmallGather:
+    def __init__(self, part, full, zs, xs, own):
+        self.part, self.full, self.zs, self.xs, self.own = part, full, zs, xs, own
+        self.x, self.y, self.z, self.c = place()
+
+    def at(self, k):
+        rows = self.part.shape[0]
+        shard = z_partner(self.z, k) * 2 + self.x
+        return pl.ds(pl.multiple_of(shard * rows, rows), rows)
+
+    def over_z(self, k):
+        target = dev(self.x, self.y, z_partner(self.z, k), self.c)
+        return remote(self.part, self.full.at[self.at(0)], self.zs.at[k - 1], target)
+
+    def over_x(self, k):
+        target = dev(1 - self.x, self.y, self.z, self.c)
+        src = self.full.at[self.at(k)] if k else self.part
+        return remote(src, self.full.at[self.at(k)], self.xs.at[k], target)
+
+    def own_copy(self):
+        return pltpu.make_async_copy(self.part, self.full.at[self.at(0)], self.own.at[0])
+
+    def step0(self):
+        for k in (1, 2, 3):
+            self.over_z(k).start()
+        self.over_x(0).start()
+        self.own_copy().start()
+
+    def step1(self):
+        for k in (1, 2, 3):
+            self.over_z(k).wait_recv()
+            self.over_x(k).start()
+
+    def step4(self):
+        for k in range(4):
+            self.over_x(k).wait()
+        for k in (1, 2, 3):
+            self.over_z(k).wait_send()
+        self.own_copy().wait()
+
+
+def dot(left, right, left_axis=1, right_axis=0):
+    return lax.dot_general(
+        left,
+        right,
+        (((left_axis,), (right_axis,)), ((), ())),
+        preferred_element_type=F32,
+    )
+
+
+def norm_parts(value):
+    center = value - jnp.mean(value, axis=-1, keepdims=True)
+    inverse = lax.rsqrt(jnp.mean(center * center, axis=-1, keepdims=True) + 1e-06)
+    return center * inverse, inverse
+
+
+def norm_back(grad, gain, hat, inverse):
+    scaled = grad * gain
+    mean = jnp.mean(scaled, axis=-1, keepdims=True)
+    return inverse * (scaled - mean - hat * jnp.mean(scaled * hat, axis=-1, keepdims=True))
+
+
+def keep_keys(scores):
+    row = lax.broadcasted_iota(jnp.int32, (LEN - CUT, scores.shape[1]), 0) + CUT
+    last = jnp.where(row < VALID, scores[CUT:], -1000000000.0)
+    return jnp.concatenate([scores[:CUT], last], axis=0)
+
+
+def by_head(value):
+    lane = lax.broadcasted_iota(jnp.int32, value.shape, 1)
+    none = jnp.zeros_like(value)
+    return jnp.where(lane < HEAD_DIM, value, none), jnp.where(lane < HEAD_DIM, none, value)
+
+
+def attend_pair(query, keys, values, store_logsum):
+    total_ctx = None
+    for i, (q, v) in enumerate(zip(by_head(query), by_head(values))):
+        scores = keep_keys(dot(keys, q, 1, 1))
+        top = jnp.max(scores, axis=0, keepdims=True)
+        expo = jnp.exp(scores - top)
+        total = jnp.sum(expo, axis=0, keepdims=True)
+        store_logsum(i, top + jnp.log(total))
+        ctx = dot((expo * (1.0 / total)).astype(LOW), v, 0, 0)
+        total_ctx = ctx if total_ctx is None else total_ctx + ctx
+    return total_ctx
+
+
+def vector_row(table, rows, first, count):
+    at = [s * rows + first + i for s in range(8) for i in range(count)]
+    pieces = [table[r : r + 1] for r in at]
+    return jnp.concatenate(pieces, axis=1)
+
+
+def front_plan(shapes):
+    (dj, cj), (do, co), (de, ce), (dr, cr) = shapes
+    plan = [(0, (0, dj, i * (cj // 3), cj // 3)) for i in range(3)]
+    plan += [(1, (0, do, 0, co))]
+    plan += [(2, (0, de, i * (ce // 4), ce // 4)) for i in range(4)]
+    plan += [(3, (i * (dr // 4), dr // 4, 0, cr)) for i in range(4)]
+    return plan
+
+
+def front_kernel(x_part, packed, wj, wo, w1, w2, *refs):
+    outs, refs = refs[:9], refs[9:]
+    fulls, (table_out, image, active, joint, ctx) = outs[:4], outs[4:]
+    (logsum, table, own_half, far_half, weight, xf, *sems) = refs
+    parts = (wj, wo, w1, w2)
+    half_sem, fetch_sem, small_sems, sems = sems[0], sems[1], sems[2:5], sems[5:]
+    x, y, z, c = place()
+    greet()
+    small = SmallGather(packed, table, *small_sems)
+    small.step0()
+    swap = remote(x_part.at[1 - c], far_half, half_sem.at[0], dev(x, y, z, 1 - c))
+    keep = pltpu.make_async_copy(x_part.at[c], own_half, half_sem.at[1, 0])
+    swap.start()
+    keep.start()
+    plan = front_plan([p.shape for p in parts])
+    pieces = [
+        Gather(parts[w], fulls[w], piece, sems, i % SLOTS) for i, (w, piece) in enumerate(plan)
+    ]
+    turns = len(pieces) + LEAD[4]
+
+    def turn(t):
+        for step in (4, 3, 2, 1, 0):
+            i = t - LEAD[step]
+            if 0 <= i < len(pieces):
+                getattr(pieces[i], f"step{step}")()
+
+    width = active.shape[1]
+    for t in range(9):
+        turn(t)
+        if t == 1:
+            small.step1()
+        if t == 2:
+            keep.wait()
+            swap.wait()
+            own, far = own_half[...].astype(F32), far_half[...].astype(F32)
+            first, second = jnp.where(c == 0, own, far), jnp.where(c == 0, far, own)
+            xf[...] = jnp.concatenate([first, second], axis=0)
+            image[...] = xf[...].astype(LOW)
+        if t == 3:
+            small.step4()
+            table_out[...] = table[...]
+            rows = packed.shape[0]
+            hat, _ = norm_parts(xf[...])
+            vectors = table[...].astype(F32)
+            gain, shift = vector_row(vectors, rows, 0, 1), vector_row(vectors, rows, 1, 1)
+            active[...] = (hat * gain + shift).astype(LOW)
+        if t >= 6:
+            cols = pl.ds((t - 6) * width, width)
+            fetch = pltpu.make_async_copy(fulls[0].at[:, cols], weight, fetch_sem.at[0])
+            fetch.start()
+            fetch.wait()
+            product = dot(active[...], weight[...])
+            if t != 7:
+                bias = vector_row(table[...].astype(F32), packed.shape[0], 2, 2)
+                product += bias[:, :width] if t == 6 else bias[:, width:]
+            joint[:, cols] = product.astype(LOW)
+
+    @pl.loop(0, turns - 9)
+    def _(t):
+        for k in range(turns - 9):
+            pl.when(t == k)(functools.partial(turn, k + 9))
+
+        @pl.when(t < width // 128)
+        def _():
+            def at(i):
+                return pl.ds(pl.multiple_of(i * width + t * 128, 128), 128)
+
+            def store(i, value):
+                logsum[t, i : i + 1, :] = value
+
+            query = joint[:, at(0)] * jnp.asarray(HEAD_DIM**-0.5, LOW)
+            ctx[:, at(0)] = attend_pair(query, joint[:, at(1)], joint[:, at(2)], store).astype(LOW)
+
+
+def front(x_part, packed, parts):
+    sds = jax.ShapeDtypeStruct
+    dma = pltpu.SemaphoreType.DMA
+    tokens, width = x_part.shape[1:]
+    pairs = width // 128
+    hbm, vmem = pl.BlockSpec(memory_space=pl.ANY), pl.BlockSpec(memory_space=pltpu.VMEM)
+    return pl.pallas_call(
+        front_kernel,
+        out_shape=[sds((p.shape[0] * 8, p.shape[1]), LOW) for p in parts]
+        + [
+            sds((packed.shape[0] * 8, 128), LOW),
+            sds((LEN, width), LOW),
+            sds((LEN, width), LOW),
+            sds((LEN, 3 * width), LOW),
+            sds((LEN, width), LOW),
+            sds((pairs, 8, LEN), F32),
+        ],
+        in_specs=[hbm] * 6,
+        out_specs=[hbm] * 4 + [vmem] * 6,
+        scratch_shapes=[
+            pltpu.VMEM((packed.shape[0] * 8, 128), LOW),
+            pltpu.VMEM((tokens, width), LOW),
+            pltpu.VMEM((tokens, width), LOW),
+            pltpu.VMEM((width, width), LOW),
+            pltpu.VMEM((LEN, width), F32),
+            dma((2, 2)),
+            dma((1,)),
+            dma((3, 2)),
+            dma((4, 2)),
+            dma((1,)),
+            dma((SLOTS, 3, 2)),
+            dma((SLOTS, 4, 2)),
+            dma((SLOTS, 8, 2)),
+            dma((SLOTS, 8, 2)),
+            dma((SLOTS, 8, 2)),
+            dma((SLOTS, 1)),
+        ],
+        compiler_params=pltpu.CompilerParams(
+            collective_id=1, has_side_effects=True, vmem_limit_bytes=VMEM_LIMIT
+        ),
+    )(x_part, packed, *parts)
+
+
+def middle_kernel(
+    chunks,
+    ctx,
+    image,
+    dout,
+    wo,
+    rows,
+    w1,
+    b1,
+    w2,
+    out,
+    hidden,
+    dupper,
+    active,
+    dattn,
+    dresid,
+    dctx,
+    small,
+    grad_b1,
+    resid,
+    total,
+    dtotal,
+):
+    j = pl.program_id(0)
+    bo, gain, shift, b2 = rows[0:1], rows[1:2], rows[2:3], rows[3:4]
+    keep = (lax.broadcasted_iota(jnp.int32, (LEN, 1), 0) < VALID).astype(F32)
+
+    @pl.when(j == 0)
+    def _():
+        attn = dot(ctx[...], wo[...]) + bo
+        value = image[...].astype(F32) + attn
+        resid[...] = value
+        hat, _ = norm_parts(value)
+        active[...] = (hat * gain + shift).astype(LOW)
+        total[...] = jnp.zeros_like(total)
+        dtotal[...] = jnp.zeros_like(dtotal)
+        small[3:4] = jnp.sum(dout[...].astype(F32), axis=0, keepdims=True)
+        small[4:5] = jnp.sum(attn * attn * keep, axis=0, keepdims=True)
+        small[7:8] = jnp.zeros_like(small[7:8])
+
+    upper = dot(active[...], w1[...]) + b1[...]
+    dhidden = dot(dout[...], w2[...], 1, 1)
+    share = 0.5 * (1.0 + lax.erf(upper * 0.7071067811865476))
+    density = jnp.exp(upper * upper * -0.5) * 0.3989422804014327
+    low = (upper * share).astype(LOW)
+    dlow = (dhidden * (share + upper * density)).astype(LOW)
+    hidden[...] = low
+    dupper[...] = dlow
+    grad_b1[...] = jnp.sum(dlow.astype(F32), axis=0, keepdims=True)
+    total[...] += dot(low, w2[...])
+    dtotal[...] += dot(dlow, w1[...], 1, 1)
+
+    @pl.when(j == chunks - 1)
+    def _():
+        branch = total[...] + b2
+        value = resid[...]
+        result = value + branch
+        out[...] = result.astype(LOW)
+        small[5:6] = jnp.sum(result * result * keep, axis=0, keepdims=True)
+        small[6:7] = jnp.sum(branch * branch * keep, axis=0, keepdims=True)
+        hat, inverse = norm_parts(value)
+        dactive = dtotal[...]
+        small[0:1] = jnp.sum(dactive * hat, axis=0, keepdims=True)
+        small[1:2] = jnp.sum(dactive, axis=0, keepdims=True)
+        grad = dout[...].astype(F32) + norm_back(dactive, gain, hat, inverse)
+        dresid[...] = grad
+        low = grad.astype(LOW)
+        dattn[...] = low
+        small[2:3] = jnp.sum(low.astype(F32), axis=0, keepdims=True)
+        dctx[...] = dot(low, wo[...], 1, 1).astype(LOW)
+
+
+def middle(ctx, image, dout, wo, rows, w1, b1, w2, step=512):
+    width, hidden = w1.shape
+    sds = jax.ShapeDtypeStruct
+    full, wide = (LEN, width), (LEN, hidden)
+
+    def whole(shape):
+        return pl.BlockSpec(shape, lambda j: (0, 0))
+
+    def by_column(size):
+        return pl.BlockSpec((size, step), lambda j: (0, j))
+
+    return pl.pallas_call(
+        functools.partial(middle_kernel, hidden // step),
+        grid=(hidden // step,),
+        in_specs=[whole(full)] * 3
+        + [whole((width, width)), whole((8, width)), by_column(width), by_column(1)]
+        + [pl.BlockSpec((step, width), lambda j: (j, 0))],
+        out_specs=[whole(full), by_column(LEN), by_column(LEN)]
+        + [whole(full)] * 4
+        + [whole((8, width)), by_column(1)],
+        out_shape=[sds(full, LOW), sds(wide, LOW), sds(wide, LOW)]
+        + [sds(full, LOW), sds(full, LOW), sds(full, F32), sds(full, LOW)]
+        + [sds((8, width), F32), sds((1, hidden), F32)],
+        scratch_shapes=[pltpu.VMEM(full, F32)] * 3,
+        compiler_params=pltpu.CompilerParams(vmem_limit_bytes=VMEM_LIMIT),
+        cost_estimate=pl.CostEstimate(
+            flops=12 * LEN * width * hidden,
+            bytes_accessed=4 * width * hidden + 4 * LEN * hidden + 24 * LEN * width,
+            transcendentals=2 * LEN * hidden,
+        ),
+    )(ctx, image, dout, wo, rows, w1, b1, w2)
+
+
+def attend_pair_back(query, keys, values, logsum, dctx):
+    heads = [by_head(v) for v in (query, keys, dctx)]
+    sums = None
+    for i in range(2):
+        q, k, d = [h[i] for h in heads]
+        probs = jnp.exp(keep_keys(dot(keys, q, 1, 1)) - logsum[i : i + 1])
+        dprobs = dot(values, d, 1, 1)
+        inner = jnp.sum(probs * dprobs, axis=0, keepdims=True)
+        dscore = (probs * (dprobs - inner)).astype(LOW)
+        grads = (dot(dscore, k, 0, 0), dot(dscore, q), dot(probs.astype(LOW), d))
+        sums = grads if sums is None else tuple(a + b for a, b in zip(sums, grads))
+    return sums
+
+
+def attention_back_kernel(query, keys, values, logsum, dctx, djoint):
+    h = pl.program_id(0)
+    factor = HEAD_DIM**-0.5
+    scaled = query[...] * jnp.asarray(factor, LOW)
+    dq, dk, dv = attend_pair_back(scaled, keys[...], values[...], logsum[0], dctx[...])
+    width = djoint.shape[1] // 3
+    for i, grad in enumerate((dq * factor, dk, dv)):
+        djoint[:, pl.ds(pl.multiple_of(i * width + h * 128, 128), 128)] = grad.astype(LOW)
+
+
+def attention_back(joint, logsum, dctx):
+    width = dctx.shape[1]
+    pairs = width // 128
+
+    def column(i):
+        return pl.BlockSpec((LEN, 128), lambda h: (0, i * pairs + h))
+
+    return pl.pallas_call(
+        attention_back_kernel,
+        grid=(pairs,),
+        in_specs=[column(0), column(1), column(2)]
+        + [pl.BlockSpec((1, 8, LEN), lambda h: (h, 0, 0)), column(0)],
+        out_specs=pl.BlockSpec((LEN, 3 * width), lambda h: (0, 0)),
+        out_shape=jax.ShapeDtypeStruct((LEN, 3 * width), LOW),
+        compiler_params=pltpu.CompilerParams(vmem_limit_bytes=VMEM_LIMIT),
+        cost_estimate=pl.CostEstimate(
+            flops=20 * LEN * LEN * width,
+            bytes_accessed=16 * LEN * width,
+            transcendentals=LEN * LEN * 2 * pairs,
+        ),
+    )(joint, joint, joint, logsum, dctx)
+
+
+def pair_perm(f):
+    pairs = []
+    for seq in range(4):
+        for shard in range(8):
+            y, c, z, x = f(seq // 2, seq % 2, shard // 2, shard % 2)
+            pairs.append((seq * 8 + shard, (y * 2 + c) * 8 + z * 2 + x))
+    return pairs
+
+
+BOTH = ("seq", "shard")
+OVER_CORE = pair_perm(lambda y, c, z, x: (y, 1 - c, z, x))
+OVER_X = pair_perm(lambda y, c, z, x: (y, c, z, 1 - x))
+OVER_Y = pair_perm(lambda y, c, z, x: (1 - y, c, z, x))
+OVER_Z = [None] + [pair_perm(lambda y, c, z, x, k=k: (y, c, z ^ k, x)) for k in (1, 2, 3)]
+
+
+def send(value, perm):
+    return lax.ppermute(value, BOTH, perm)
+
+
+def pick(value, index, axis):
+    return lax.dynamic_index_in_dim(value, index, axis, keepdims=False)
+
+
+def add_low(left, right):
+    return (left.astype(F32) + right.astype(F32)).astype(LOW)
+
+
+def partial_grad(left, right):
+    c = place()[3]
+    tokens, rows = left.shape
+    split = left.reshape(tokens, 2, 2, rows // 4)
+
+    def part(core):
+        return dot(pick(split, core, 2).reshape(tokens, rows // 2), right, 0, 0).astype(LOW)
+
+    return part(1 - c), part(c)
+
+
+def scatter_grad(theirs, low):
+    x, y, z, c = place()
+    rows, cols = low.shape
+    low = add_low(low, send(theirs, OVER_CORE))
+    low = low.reshape(2, 4, 2, rows // 16, cols)
+    half = cols // 2
+    first, second = low[..., :half], low[..., half:]
+    got_first = send(pick(first, 1 - y, 0), OVER_Y)
+    got_second = send(pick(second, 1 - x, 2), OVER_X)
+    first = add_low(pick(first, y, 0), got_first)
+    second = add_low(pick(second, x, 2), got_second)
+    got_first = send(pick(first, 1 - x, 1), OVER_X)
+    got_second = send(pick(second, 1 - y, 0), OVER_Y)
+    first = pick(first, x, 1).astype(F32) + got_first.astype(F32)
+    second = pick(second, y, 0).astype(F32) + got_second.astype(F32)
+    whole = jnp.concatenate([first, second], axis=-1)
+    low = whole.astype(LOW)
+    total = pick(whole, z, 0)
+    for k in (1, 2, 3):
+        total += send(pick(low, z_partner(z, k), 0), OVER_Z[k]).astype(F32)
+    return total
+
+
+def sum_everywhere(value):
+    for perm in (OVER_CORE, OVER_X, OVER_Y, OVER_Z[1], OVER_Z[2]):
+        value = value + send(value, perm)
+    return value
+
+
+def on_chip(
+    inputs,
+    cotangent,
+    first_gain,
+    first_shift,
+    joint_weight,
+    joint_bias,
+    output_weight,
+    output_bias,
+    second_gain,
+    second_shift,
+    expand_weight,
+    expand_bias,
+    reduce_weight,
+    reduce_bias,
+):
+    c = place()[3]
+    tokens, width = inputs.shape[1:]
+    smalls = [
+        first_gain,
+        first_shift,
+        joint_bias,
+        output_bias,
+        second_gain,
+        second_shift,
+        expand_bias,
+        reduce_bias,
+    ]
+    packed = jnp.concatenate([v.reshape(-1, 128) for v in smalls])
+    packed = jnp.pad(packed, ((0, -packed.shape[0] % 16), (0, 0)))
+
+    def whole_image(value):
+        own, got = pick(value, c, 0), send(pick(value, 1 - c, 0), OVER_CORE)
+        return jnp.concatenate([jnp.where(c == 0, own, got), jnp.where(c == 0, got, own)])
+
+    def own_tokens(value):
+        parts = value.reshape(2, tokens, width)
+        own, got = pick(parts, c, 0), send(pick(parts, 1 - c, 0), OVER_CORE)
+        return jnp.stack([jnp.where(c == 0, own, got), jnp.where(c == 0, got, own)])
+
+    keep = jnp.arange(LEN, dtype=jnp.int32)[:, None] < VALID
+    dout = jnp.where(keep, whole_image(cotangent), 0)
+    wj, wo, w1, w2, vectors, image, active1, joint, context, logsum = front(
+        inputs, packed, (joint_weight, output_weight, expand_weight, reduce_weight)
+    )
+    vectors = vectors.reshape(8, -1, 128).astype(F32)
+    fulls, at = [], 0
+    for v in smalls:
+        rows = v.shape[0] // 128
+        fulls.append(vectors[:, at : at + rows].reshape(-1))
+        at += rows
+    g1, s1, bj, bo, g2, s2, b1, b2 = fulls
+    rows = jnp.pad(jnp.stack([bo, g2, s2, b2]), ((0, 4), (0, 0)))
+    result, hidden, dupper, active2, dattn, dresid, dcontext, small, grad_b1 = middle(
+        context, image, dout, wo, rows, w1, b1[None], w2
+    )
+    parts_w2 = partial_grad(hidden, dout)
+    parts_w1 = partial_grad(active2, dupper)
+    parts_wo = partial_grad(context, dattn)
+    parts_w2, parts_w1, parts_wo, dcontext = lax.optimization_barrier(
+        (parts_w2, parts_w1, parts_wo, dcontext)
+    )
+    own_w2, own_w1, own_wo = [scatter_grad(*p) for p in (parts_w2, parts_w1, parts_wo)]
+    layer_out = own_tokens(result)
+    djoint = attention_back(joint, logsum, dcontext)
+    parts_wj = partial_grad(active1, djoint)
+    own_wj = scatter_grad(*parts_wj)
+    joint_sums = jnp.sum(djoint.astype(F32), axis=0)
+    dactive = dot(djoint, wj, 1, 1)
+    hat, inverse = norm_parts(image.astype(F32))
+    grad_g1, grad_s1 = jnp.sum(dactive * hat, axis=0), jnp.sum(dactive, axis=0)
+    dimage = dresid + norm_back(dactive, g1, hat, inverse)
+    input_grad = own_tokens(dimage.astype(LOW))
+    counted = jnp.full((1,), VALID * width, F32)
+    grads = [grad_g1, grad_s1, joint_sums[:width], joint_sums[2 * width :]]
+    grads += [small[2], small[0], small[1], grad_b1[0], small[3]]
+    sums = [jnp.sum(small[i])[None] for i in (5, 4, 6)] + [counted]
+    totals = sum_everywhere(jnp.concatenate(grads + sums + [jnp.zeros((124,), F32)]))
+    rank = lax.axis_index("seq") * 8 + lax.axis_index("shard")
+    own, at = [], 0
+    for v in smalls:
+        size = v.shape[0] * 8
+        own.append(lax.dynamic_slice(totals, (at + rank * (size // 32),), (size // 32,)))
+        at += size
+    own_g1, own_s1, own_bj, own_bo, own_g2, own_s2, own_b1, own_b2 = own
+    root_means = jnp.sqrt(totals[at : at + 3] / totals[at + 3] + 1e-06)
+    return (
+        layer_out,
+        input_grad,
+        own_g1,
+        own_s1,
+        own_wj,
+        own_bj,
+        own_wo,
+        own_bo,
+        own_g2,
+        own_s2,
+        own_w1,
+        own_b1,
+        own_w2,
+        own_b2,
+        root_means,
+    )
+
+
 def solution(mesh):
+    whole_images = mesh.shape["seq"] == 4 and mesh.shape["shard"] == 8
     return jax.shard_map(
-        on_device,
+        on_chip if whole_images else on_device,
         mesh=mesh,
         in_specs=(
             P("shard", "seq", None),

time: 1550 us -> 523 us (0.34)
  waiting for transfers between devices: 891 us -> 104 us
  blocking collectives: 246 us -> 0 us
  Pallas kernels: 0 us -> 184 us
  matrix products: 178 us -> 45.4 us
  local copies, waits for them, and re-layouts: 145 us -> 103 us
  starting transfers between devices: 13.3 us -> 49.1 us
  other arithmetic: 55.2 us -> 26.9 us
    reduce_scatter x4 -> x0, waiting for transfers between devices: 777 us -> none  [the longest x1 360 us: on_device(): lax.psum_scatter(grad_w2, ('seq', 'shard'), scatter_dimension=0, tiled=True)]
    pallas_call x0 -> x3, Pallas kernels: none -> 184 us  [the longest x1 118 us: front(): pl.pallas_call(front_kernel, out_shape=[sds((p.shape[0] * 8, p.shape[1]),...]
    all_gather x8 -> x0, blocking collectives: 153 us -> none  [the longest x1 26.3 us: on_device(): lax.all_gather(expand_bias, 'shard', axis=0, tiled=True)]
    dot_general x40 -> x9, matrix products: 178 us -> 45.4 us  [dot(): lax.dot_general(left, right, (((left_axis,), (right_axis,)), ((), ())), p...]
    ppermute x0 -> x40, waiting for transfers between devices: none -> 104 us  [send(): return lax.ppermute(value, BOTH, perm)]
    all_to_all x3 -> x0, waiting for transfers between devices: 69.1 us -> none  [the longest x1 53.2 us: on_device(): lax.all_to_all(joint, 'seq', split_axis=3, concat_axis=1, tiled=True)]
    dynamic_slice x0 -> x11, local copies, waits for them, and re-layouts: none -> 64.2 us  [the longest x8 62.5 us: pick(): return lax.dynamic_index_in_dim(value, index, axis, keepdims=False)]
    all_to_all x1 -> x0, blocking collectives: 51.4 us -> none  [on_device(): lax.all_to_all(dheads, 'seq', split_axis=1, concat_axis=3, tiled=True)]
  transfers between devices with their start and end apart: 11 -> 40, of which waited for: 6 -> 23; matrix products, arithmetic and copies ran while one was open for 21% -> 12% of each run, Pallas kernels for 0% -> 23%
where the time goes in v1:
time: 523 us; the launch traced here: 514 us
  Pallas kernels  184 us (35%)
  waiting for transfers between devices  104 us (20%)
  local copies, waits for them, and re-layouts  103 us (20%)
  starting transfers between devices  49.1 us (9%)
  matrix products  45.4 us (9%)
  other arithmetic  26.9 us (5%)
    pallas_call x1, Pallas kernels, front(): pl.pallas_call(front_kernel, out_shape=[sds((p.shape[0] * 8, p.shape[1]),...  118 us
    ppermute x40, waiting for transfers between devices, send(): return lax.ppermute(value, BOTH, perm)  104 us
    dynamic_slice x8, local copies, waits for them, and re-layouts, pick(): return lax.dynamic_index_in_dim(value, index, axis, keepdims=False)  62.5 us
    ppermute x40, starting transfers between devices, send(): return lax.ppermute(value, BOTH, perm)  49.1 us
    dot_general x9, matrix products, dot(): lax.dot_general(left, right, (((left_axis,), (right_axis,)), ((), ())), p...  45.4 us
    pallas_call x1, Pallas kernels, middle(): pl.pallas_call(functools.partial(middle_kernel, hidden // step), grid=(hi...  35.5 us
    pallas_call x1, Pallas kernels, attention_back(): pl.pallas_call(attention_back_kernel, grid=(pairs,), in_specs=[column(0),...  30.4 us
    reshape x4, local copies, waits for them, and re-layouts, partial_grad(): split = left.reshape(tokens, 2, 2, rows // 4)  17.9 us
  transfers between devices with their start and end apart: 40, of which 23 were waited for; matrix products, arithmetic and copies ran while one was open for 12% of the time, Pallas kernels for 23%

profile of v1, /device:TPU:0, one launch (start us, length us, event | category | flops | bytes accessed | tf_op | source)
XLA Modules:
  0.0 513.5 jit_solution(7540717323807056518)
XLA Ops:
  0.7 1.9 dynamic-slice_bitcast_fusion.5
  3.0 2.2 concatenate.21
  5.9 118.1 %shard_map.253 = (bf16[1024,3072]{1,0:T(8,128)(2,1)}, bf16[1024,1024]{1,0:T(8,128)(2,1)}, bf16[1024,4096]{1,0:T(8,128)(2,1)}, bf16[4096,1024]{1,0:T(8,128)(2,1)}...) custom-call(bf16[2,296,1024]{2,1,0:T(8,128)(2,1)} %x_part.1, ...), custom_call_target="tpu_custom_call" | custom-call | tf_op jit(solution)/shard_map/pallas_call | solution.py:566
  124.7 1.4 slice.104
  126.8 1.5 convert_reduce_fusion.1
  128.3 3.6 reshape.192
  131.9 8.4 %dynamic-slice_reduce_fusion.4 = (bf16[592,2,256]{2,1,0:T(2,128)(2,1)S(1)}, bf16[592,2,256]{2,1,0:T(2,128)(2,1)S(1)}) fusion(bf16[592,2,2,256]{3,2,1,0:T(2,128)(2,1)S(1)} %reshape.192, s32[]{:T(128)S(6)} %select_n.166, s32[]{:T(128)S(6)} %select_n.167), kind=kLoop, calls=%fused_computation.59 | loop fusion | bytes 2424840 | tf_op jit(solution)/shard_map/jit(dynamic_index_in_dim)/dynamic_slice | solution.py:776
  142.2 1.3 reshape.196
  143.6 8.4 %dynamic-slice_reduce_fusion.3 = (bf16[592,2,256]{2,1,0:T(2,128)(2,1)S(1)}, bf16[592,2,256]{2,1,0:T(2,128)(2,1)S(1)}) fusion(bf16[592,2,2,256]{3,2,1,0:T(2,128)(2,1)S(1)} %reshape.196, s32[]{:T(128)S(6)} %select_n.166, s32[]{:T(128)S(6)} %select_n.167), kind=kLoop, calls=%fused_computation.58 | loop fusion | bytes 2424840 | tf_op jit(solution)/shard_map/jit(dynamic_index_in_dim)/dynamic_slice | solution.py:776
  155.3 1.3 maximum_select_fusion.dout
  156.6 35.5 %shard_map.254 = (bf16[592,1024]{1,0:T(8,128)(2,1)}, bf16[592,4096]{1,0:T(8,128)(2,1)}, bf16[592,4096]{1,0:T(8,128)(2,1)}, bf16[592,1024]{1,0:T(8,128)(2,1)}, bf...) custom-call(bf16[592,1024]{1,0:T(8,128)(2,1)} %get-tuple-element.41., ...), custom_call_target="tpu_custom_call" | custom-call | flops 29796335616 | bytes 41025536 | tf_op jit(solution)/shard_map/pallas_call | solution.py:686
  192.1 1.6 slice_reduce_fusion
  193.8 3.3 convolution_convert_fusion.7
  197.1 2.0 convolution_convert_fusion.6
  200.2 8.4 %dynamic-slice_reduce_fusion.6 = (bf16[592,2,256]{2,1,0:T(2,128)(2,1)S(1)}, bf16[592,2,256]{2,1,0:T(2,128)(2,1)S(1)}) fusion(bf16[592,2,2,256]{3,2,1,0:T(2,128)(2,1)S(1)} %reshape.189, s32[]{:T(128)S(6)} %select_n.166, s32[]{:T(128)S(6)} %select_n.167), kind=kLoop, calls=%fused_computation.61 | loop fusion | bytes 2424840 | tf_op jit(solution)/shard_map/jit(dynamic_index_in_dim)/dynamic_slice | solution.py:776
  208.8 7.7 %convolution_convert_fusion.1 = bf16[512,4096]{1,0:T(8,128)(2,1)} fusion(bf16[592,512]{1,0:T(8,128)(2,1)S(1)} %bitcast.274, bf16[592,4096]{1,0:T(8,128)(2,1)} %get-tuple-element.53), kind=kOutput, calls=%fused_computation.5 | convolution fusion | flops 2485125120 | bytes 9650176 | tf_op jit(solution)/shard_map/dot_general | solution.py:426
  216.5 5.5 %convolution_convert_fusion = bf16[512,4096]{1,0:T(8,128)(2,1)} fusion(bf16[592,512]{1,0:T(8,128)(2,1)S(1)} %bitcast.273, bf16[592,4096]{1,0:T(8,128)(2,1)S(1)} %bitcast.296), kind=kOutput, calls=%fused_computation.4 | convolution fusion | flops 2485125120 | bytes 9650176 | tf_op jit(solution)/shard_map/dot_general | solution.py:426
  221.9 11.9 %reshape.186 = bf16[592,2,2,1024]{3,2,1,0:T(2,128)(2,1)} reshape(bf16[592,4096]{1,0:T(8,128)(2,1)} %get-tuple-element.51) | data formatting | bytes 9699328 | tf_op jit(solution)/shard_map/reshape | solution.py:786
  233.8 36.9 %dynamic-slice_reduce_fusion = (bf16[592,2,1024]{2,1,0:T(2,128)(2,1)}, bf16[592,2,1024]{2,1,0:T(2,128)(2,1)S(1)}) fusion(bf16[592,2,2,1024]{3,2,1,0:T(2,128)(2,1)} %reshape.186, s32[]{:T(128)S(6)} %select_n.166, s32[]{:T(128)S(6)} %select_n.167), kind=kLoop, calls=%fused_computation.6 | loop fusion | bytes 9699336 | tf_op jit(solution)/shard_map/jit(dynamic_index_in_dim)/dynamic_slice | solution.py:776
  270.7 2.4 copy.66
  274.4 5.0 convolution_convert_fusion.5
  279.4 5.1 convolution_convert_fusion.4
  284.5 30.4 %shard_map.255 = bf16[592,3072]{1,0:T(8,128)(2,1)} custom-call(bf16[592,3072]{1,0:T(8,128)(2,1)} %get-tuple-element.49.query.keys.values, bf16[592,3072]{1,0:T(8,128)(2,1)} %get-tuple-element.49.query.keys.values, bf16[592,3072]{1,0:T(8,128)(2,1)} %get-tuple-element.49.query.keys.values, f32[8,8,592]{2,1,0:T(8,128)} %get-tuple-element.50.logsum, ...), custom_call_target="tpu_custom_call" | custom-call | flops 7177502720 | bytes 9699328 | tf_op jit(solution)/shard_map/pallas_call | solution.py:739
  314.9 2.9 convert_reduce_fusion
  318.1 8.8 %fusion.10 = (f32[1024]{0:T(1024)S(1)}, f32[592]{0:T(1024)S(1)}, f32[592]{0:T(1024)S(1)}, f32[1024]{0:T(1024)S(1)}, f32[592,1024]{1,0:T(8,128)}) fusion(bf16[592,1024]{1,0:T(8,128)(2,1)S(1)} %copy-done.3, f32[592]{0:T(1024)S(1)} %add_rsqrt_fusion, f32[592]{0:T(1024)S(1)} %broadcast_multiply_fusion.2, f32[1024]{0:T(1024)S(1)} %bitcast.279, ...), kind=kOutput, calls=%fused_computation.30 | convolution fusion | flops 3730600960 | bytes 13587712 | tf_op jit(solution)/shard_map/dot_general | solution.py:426
  326.8 2.0 concatenate.23
  331.4 5.0 convolution_convert_fusion.2
  336.6 4.2 collective-permute-done.5
  340.8 2.3 collective-permute-start.6
  345.2 4.6 collective-permute-start.7
  350.0 2.4 collective-permute-done.7
  359.1 1.6 collective-permute-start.17
  360.7 5.8 %collective-permute-done.19 = bf16[2,4,32,512]{3,2,1,0:T(8,128)(2,1)S(1)} collective-permute-done((bf16[2,4,32,512]{3,2,1,0:T(8,128)(2,1)S(1)}, bf16[2,4,32,512]{3,2,1,0:T(8,128)(2,1)S(1)}, u32[]{:S(2)}, u32[]{:S(2)}) %collective-permute-start.19) | collective-permute-done | bytes 262176 | tf_op jit(solution)/shard_map/ppermute | solution.py:772
  366.6 1.6 collective-permute-start.20
  368.2 1.5 collective-permute-start.18
  369.7 2.0 collective-permute-done.20
  371.8 1.5 collective-permute-done.18
  373.3 3.1 add_convert_fusion.2
  376.9 1.5 collective-permute-start.11
  379.7 4.1 collective-permute-start.23
  383.8 1.8 collective-permute-start.22
  386.1 1.7 collective-permute-start.9
  389.6 5.4 %collective-permute-done.11 = bf16[2,4,32,1536]{3,2,1,0:T(8,128)(2,1)S(1)} collective-permute-done((bf16[2,4,32,1536]{3,2,1,0:T(8,128)(2,1)S(1)}, bf16[2,4,32,1536]{3,2,1,0:T(8,128)(2,1)S(1)}, u32[]{:S(2)}, u32[]{:S(2)}) %collective-permute-start.11) | collective-permute-done | bytes 786464 | tf_op jit(solution)/shard_map/ppermute | solution.py:772
  395.3 1.3 collective-permute-start.12
  396.6 10.0 %collective-permute-done.9 = bf16[4,2,32,1536]{3,2,0,1:T(8,128)(2,1)S(1)} collective-permute-done((bf16[4,2,32,1536]{3,2,0,1:T(8,128)(2,1)S(1)}, bf16[4,2,32,1536]{3,2,0,1:T(8,128)(2,1)S(1)}, u32[]{:S(2)}, u32[]{:S(2)}) %collective-permute-start.9) | collective-permute-done | bytes 786464 | tf_op jit(solution)/shard_map/ppermute | solution.py:772
  408.4 1.8 add_convert_fusion.1
  412.3 1.7 collective-permute-start.25
  414.1 2.2 add_convert_fusion
  417.0 3.0 collective-permute-done.10
  422.4 2.7 collective-permute-start.15
  427.8 3.1 collective-permute-done.15
  430.9 1.7 collective-permute-start.33
  432.6 2.9 collective-permute-done.14
  436.4 5.9 %collective-permute-done.27 = bf16[2,4,32,2048]{3,2,1,0:T(8,128)(2,1)S(1)} collective-permute-done((bf16[2,4,32,2048]{3,2,1,0:T(8,128)(2,1)S(1)}, bf16[2,4,32,2048]{3,2,1,0:T(8,128)(2,1)S(1)}, u32[]{:S(2)}, u32[]{:S(2)}) %collective-permute-start.27) | collective-permute-done | bytes 1048608 | tf_op jit(solution)/shard_map/ppermute | solution.py:772
  442.8 1.8 collective-permute-start.28
  445.4 19.4 %collective-permute-done.35 = bf16[2,4,128,512]{3,2,1,0:T(8,128)(2,1)S(1)} collective-permute-done((bf16[2,4,128,512]{3,2,1,0:T(8,128)(2,1)S(1)}, bf16[2,4,128,512]{3,2,1,0:T(8,128)(2,1)S(1)}, u32[]{:S(2)}, u32[]{:S(2)}) %collective-permute-start.35) | collective-permute-done | bytes 1048608 | tf_op jit(solution)/shard_map/ppermute | solution.py:772
  465.2 1.8 collective-permute-start.36
  467.7 4.4 collective-permute-done.28
  472.9 3.6 collective-permute-start.31
  477.0 1.3 collective-permute-done.36
  479.0 3.6 collective-permute-start.39
  482.6 7.0 %collective-permute-done.29 = bf16[32,4096]{1,0:T(8,128)(2,1)S(1)} collective-permute-done((bf16[32,4096]{1,0:T(8,128)(2,1)S(1)}, bf16[32,4096]{1,0:T(8,128)(2,1)S(1)}, u32[]{:S(2)}, u32[]{:S(2)}) %collective-permute-start.29) | collective-permute-done | bytes 262176 | tf_op jit(solution)/shard_map/ppermute | solution.py:772
  490.3 16.2 %collective-permute-done.30 = bf16[32,4096]{1,0:T(8,128)(2,1)S(1)} collective-permute-done((bf16[32,4096]{1,0:T(8,128)(2,1)S(1)}, bf16[32,4096]{1,0:T(8,128)(2,1)S(1)}, u32[]{:S(2)}, u32[]{:S(2)}) %collective-permute-start.30) | collective-permute-done | bytes 262176 | tf_op jit(solution)/shard_map/ppermute | solution.py:772
  507.5 4.7 collective-permute-done.38
  (182 shorter events, 43.8 us)
Async XLA Ops:
  2.6 151.5 %collective-permute-start = (bf16[296,1024]{1,0:T(8,128)(2,1)}, bf16[296,1024]{1,0:T(8,128)(2,1)}, u32[]{:S(2)}, u32[]{:S(2)}) collective-permute-start(bf16[296,1024]{1,0:T(8,128)(2,1)} %dynamic-slice_bitcast_fusion.5), channel_id=1, source_target_pairs={{0,8},{1,9},{2,10},{3,11},{4,12},{5,13},{6,14},{7,15},{8,0},{9,1},... | collective-permute-start | bytes 1818632 | tf_op jit(solution)/shard_map/ppermute | solution.py:772
  140.3 1.9 copy-start.8
  143.5 10.1 %copy-start.2 = (bf16[592,1024]{1,0:T(8,128)(2,1)S(1)}, bf16[592,1024]{1,0:T(8,128)(2,1)}, u32[]{:S(2)}) copy-start(bf16[592,1024]{1,0:T(8,128)(2,1)} %get-tuple-element.42.image) | copy-start | bytes 3637252
  151.9 2.2 copy-start.11
  156.6 37.2 %copy-start.16 = (bf16[74,8,2,256]{3,1,2,0:T(8,128)(2,1)S(1)}, bf16[74,8,2,256]{3,1,2,0:T(8,128)(2,1)}, u32[]{:S(2)}) copy-start(bf16[74,8,2,256]{3,1,2,0:T(8,128)(2,1)} %copy.69) | copy-start | bytes 1818628
  192.1 4.9 copy-start.15
  192.1 4.9 copy-start.19
  197.0 2.0 copy-start.10
  208.6 7.8 %slice-start = ((s8[4849664]{0:T(1024)(128)(4,1)}), s8[4194304]{0:T(1024)(128)(4,1)S(1)}, s32[]{:S(2)}) async-start(s8[4849664]{0:T(1024)(128)(4,1)} %bitcast.295), calls=%async_computation | async-start | bytes 8388608
  208.8 7.7 %slice-start.1 = ((s8[4849664]{0:T(1024)(128)(4,1)}), s8[655360]{0:T(1024)(128)(4,1)S(1)}, s32[]{:S(2)}) async-start(s8[4849664]{0:T(1024)(128)(4,1)} %bitcast.295), calls=%async_computation.1 | async-start | bytes 1310720
  273.1 1.3 copy-start.9
  284.5 33.4 %copy-start.3 = (bf16[592,1024]{1,0:T(8,128)(2,1)S(1)}, bf16[592,1024]{1,0:T(8,128)(2,1)}, u32[]{:S(2)}) copy-start(bf16[592,1024]{1,0:T(8,128)(2,1)} %get-tuple-element.42.image) | copy-start | bytes 3637252
  314.9 3.1 copy-start
  318.1 8.8 %copy-start.17 = (f32[1,4096]{1,0:T(1,128)S(1)}, f32[1,4096]{1,0:T(1,128)}, u32[]{:S(2)}) copy-start(f32[1,4096]{1,0:T(1,128)} %get-tuple-element.59) | copy-start | bytes 49156
  318.1 10.8 %copy-start.12 = (bf16[592,1024]{1,0:T(8,128)(2,1)S(1)}, bf16[592,1024]{1,0:T(8,128)(2,1)}, u32[]{:S(2)}) copy-start(bf16[592,1024]{1,0:T(8,128)(2,1)} %get-tuple-element.47) | copy-start | bytes 3637252
  328.9 1.2 collective-permute-start.3
  328.9 26.9 %collective-permute-start.1 = (bf16[296,1024]{1,0:T(8,128)(2,1)S(1)}, bf16[296,1024]{1,0:T(8,128)(2,1)S(1)}, u32[]{:S(2)}, u32[]{:S(2)}) collective-permute-start(bf16[296,1024]{1,0:T(8,128)(2,1)S(1)} %dynamic-slice_bitcast_fusion.4), channel_id=1, source_target_pairs={{0,8},{1,9},{2,10},{3,11},{4,12},{5,13},{6,14},{7,15},{8,0},{9,1},... | collective-permute-start | bytes 1818632 | tf_op jit(solution)/shard_map/ppermute | solution.py:772
  329.5 27.1 %collective-permute-start.16 = (bf16[512,1024]{1,0:T(8,128)(2,1)}, bf16[512,1024]{1,0:T(8,128)(2,1)S(1)}, u32[]{:S(2)}, u32[]{:S(2)}) collective-permute-start(bf16[512,1024]{1,0:T(8,128)(2,1)} %convolution_convert_fusion.7), channel_id=1, source_target_pairs={{0,8},{1,9},{2,10},{3,11},{4,12},{5,13},{6,14},{7,15},{8,0},{9,1},... | collective-permute-start | bytes 3145736 | tf_op jit(solution)/shard_map/ppermute | solution.py:772
  330.1 6.4 %collective-permute-start.4 = (f32[12416]{0:T(1024)S(1)}, f32[12416]{0:T(1024)S(1)}, u32[]{:S(2)}, u32[]{:S(2)}) collective-permute-start(f32[12416]{0:T(1024)S(1)} %add.303), channel_id=1, source_target_pairs={{0,1},{1,0},{2,3},{3,2},{4,5},{5,4},{6,7},{7,6},{8,9},{9,8},{10,11... | collective-permute-start | bytes 149000 | tf_op jit(solution)/shard_map/ppermute | solution.py:772
  331.4 11.7 %copy-start.6 = (f32[592,1024]{1,0:T(8,128)S(1)}, f32[592,1024]{1,0:T(8,128)}, u32[]{:S(2)}) copy-start(f32[592,1024]{1,0:T(8,128)} %get-tuple-element.48) | copy-start | bytes 7274500
  331.4 11.7 %copy-start.7 = (f32[592,1024]{1,0:T(8,128)S(1)}, f32[592,1024]{1,0:T(8,128)}, u32[]{:S(2)}) copy-start(f32[592,1024]{1,0:T(8,128)} %get-tuple-element.132) | copy-start | bytes 7274500
  336.4 36.9 %collective-permute-start.8 = (bf16[512,3072]{1,0:T(8,128)(2,1)S(1)}, bf16[512,3072]{1,0:T(8,128)(2,1)S(1)}, u32[]{:S(2)}, u32[]{:S(2)}) collective-permute-start(bf16[512,3072]{1,0:T(8,128)(2,1)S(1)} %convolution_convert_fusion.2), channel_id=1, source_target_pairs={{0,8},{1,9},{2,10},{3,11},{4,12},{5,13},{6,14},{7,15},{8,0},{9,1},... | collective-permute-start | bytes 9437192 | tf_op jit(solution)/shard_map/ppermute | solution.py:772
  336.5 4.3 collective-permute-start.5
  340.8 4.4 collective-permute-start.6
  343.1 9.2 %copy-start.18 = (bf16[512,4096]{1,0:T(8,128)(2,1)S(1)}, bf16[512,4096]{1,0:T(8,128)(2,1)}, u32[]{:S(2)}) copy-start(bf16[512,4096]{1,0:T(8,128)(2,1)} %convolution_convert_fusion.1) | copy-start | bytes 12582916
  343.1 13.3 %copy-start.13 = (bf16[592,1024]{1,0:T(8,128)(2,1)S(1)}, bf16[592,1024]{1,0:T(8,128)(2,1)}, u32[]{:S(2)}) copy-start(bf16[592,1024]{1,0:T(8,128)(2,1)} %get-tuple-element.47) | copy-start | bytes 3637252
  345.2 7.1 %collective-permute-start.7 = (f32[12416]{0:T(1024)S(1)}, f32[12416]{0:T(1024)S(1)}, u32[]{:S(2)}, u32[]{:S(2)}) collective-permute-start(f32[12416]{0:T(1024)S(1)} %add.306), channel_id=1, source_target_pairs={{0,4},{1,5},{2,6},{3,7},{4,0},{5,1},{6,2},{7,3},{8,12},{9,13},{10,... | collective-permute-start | bytes 149000 | tf_op jit(solution)/shard_map/ppermute | solution.py:772
  349.9 6.6 %collective-permute-start.2 = (bf16[296,1024]{1,0:T(8,128)(2,1)S(1)}, bf16[296,1024]{1,0:T(8,128)(2,1)S(1)}, u32[]{:S(2)}, u32[]{:S(2)}) collective-permute-start(bf16[296,1024]{1,0:T(8,128)(2,1)S(1)} %dynamic-slice_bitcast_fusion.3), channel_id=1, source_target_pairs={{0,8},{1,9},{2,10},{3,11},{4,12},{5,13},{6,14},{7,15},{8,0},{9,1},... | collective-permute-start | bytes 1818632 | tf_op jit(solution)/shard_map/ppermute | solution.py:772
  352.3 56.1 %collective-permute-start.24 = (bf16[512,4096]{1,0:T(8,128)(2,1)S(1)}, bf16[512,4096]{1,0:T(8,128)(2,1)S(1)}, u32[]{:S(2)}, u32[]{:S(2)}) collective-permute-start(bf16[512,4096]{1,0:T(8,128)(2,1)S(1)} %copy-done.18), channel_id=1, source_target_pairs={{0,8},{1,9},{2,10},{3,11},{4,12},{5,13},{6,14},{7,15},{8,0},{9,1},... | collective-permute-start | bytes 12582920 | tf_op jit(solution)/shard_map/ppermute | solution.py:772
  355.9 1.2 copy-start.14
  355.9 58.2 %collective-permute-start.32 = (bf16[2048,1024]{1,0:T(8,128)(2,1)}, bf16[2048,1024]{1,0:T(8,128)(2,1)S(1)}, u32[]{:S(2)}, u32[]{:S(2)}) collective-permute-start(bf16[2048,1024]{1,0:T(8,128)(2,1)} %convolution_convert_fusion.5), channel_id=1, source_target_pairs={{0,8},{1,9},{2,10},{3,11},{4,12},{5,13},{6,14},{7,15},{8,0},{9,1},... | collective-permute-start | bytes 12582920 | tf_op jit(solution)/shard_map/ppermute | solution.py:772
  357.7 8.8 %collective-permute-start.19 = (bf16[2,4,32,512]{3,2,1,0:T(8,128)(2,1)S(1)}, bf16[2,4,32,512]{3,2,1,0:T(8,128)(2,1)S(1)}, u32[]{:S(2)}, u32[]{:S(2)}) collective-permute-start(bf16[2,4,32,512]{3,2,1,0:T(8,128)(2,1)S(1)} %dynamic-slice_bitcast_fusion.18), channel_id=1, source_target_pairs={{0,1},{1,0},{2,3},{3,2},{4,5},{5,4},{6,7},{7,6},{8,9},{9,8},{10,11... | collective-permute-start | bytes 786440 | tf_op jit(solution)/shard_map/ppermute | solution.py:772
  359.0 14.3 %copy-start.1 = (bf16[592,3072]{1,0:T(8,128)(2,1)S(1)}, bf16[592,3072]{1,0:T(8,128)(2,1)}, u32[]{:S(2)}) copy-start(bf16[592,3072]{1,0:T(8,128)(2,1)} %shard_map.255) | copy-start | bytes 10911748
  359.1 9.1 %collective-permute-start.17 = (bf16[4,2,32,512]{3,2,0,1:T(8,128)(2,1)S(1)}, bf16[4,2,32,512]{3,2,0,1:T(8,128)(2,1)S(1)}, u32[]{:S(2)}, u32[]{:S(2)}) collective-permute-start(bf16[4,2,32,512]{3,2,0,1:T(8,128)(2,1)S(1)} %bitcast.275), channel_id=1, source_target_pairs={{0,16},{1,17},{2,18},{3,19},{4,20},{5,21},{6,22},{7,23},{8,24},{9,... | collective-permute-start | bytes 786440 | tf_op jit(solution)/shard_map/ppermute | solution.py:772
  366.6 5.2 %collective-permute-start.20 = (bf16[4,32,512]{2,1,0:T(8,128)(2,1)S(1)}, bf16[4,32,512]{2,1,0:T(8,128)(2,1)S(1)}, u32[]{:S(2)}, u32[]{:S(2)}) collective-permute-start(bf16[4,32,512]{2,1,0:T(8,128)(2,1)S(1)} %dynamic-slice_bitcast_fusion.22), channel_id=1, source_target_pairs={{0,16},{1,17},{2,18},{3,19},{4,20},{5,21},{6,22},{7,23},{8,24},{9,... | collective-permute-start | bytes 393224 | tf_op jit(solution)/shard_map/ppermute | solution.py:772
  368.2 5.0 collective-permute-start.18
  376.9 18.1 %collective-permute-start.11 = (bf16[2,4,32,1536]{3,2,1,0:T(8,128)(2,1)S(1)}, bf16[2,4,32,1536]{3,2,1,0:T(8,128)(2,1)S(1)}, u32[]{:S(2)}, u32[]{:S(2)}) collective-permute-start(bf16[2,4,32,1536]{3,2,1,0:T(8,128)(2,1)S(1)} %dynamic-slice_bitcast_fusion.2), channel_id=1, source_target_pairs={{0,1},{1,0},{2,3},{3,2},{4,5},{5,4},{6,7},{7,6},{8,9},{9,8},{10,11... | collective-permute-start | bytes 2359304 | tf_op jit(solution)/shard_map/ppermute | solution.py:772
  378.5 5.3 %collective-permute-start.21 = (bf16[32,1024]{1,0:T(8,128)(2,1)S(1)}, bf16[32,1024]{1,0:T(8,128)(2,1)S(1)}, u32[]{:S(2)}, u32[]{:S(2)}) collective-permute-start(bf16[32,1024]{1,0:T(8,128)(2,1)S(1)} %get-tuple-element.113), channel_id=1, source_target_pairs={{0,2},{1,3},{2,0},{3,1},{4,6},{5,7},{6,4},{7,5},{8,10},{9,11},{10,... | collective-permute-start | bytes 196616 | tf_op jit(solution)/shard_map/ppermute | solution.py:772
  379.7 6.5 %collective-permute-start.23 = (bf16[32,1024]{1,0:T(8,128)(2,1)S(1)}, bf16[32,1024]{1,0:T(8,128)(2,1)S(1)}, u32[]{:S(2)}, u32[]{:S(2)}) collective-permute-start(bf16[32,1024]{1,0:T(8,128)(2,1)S(1)} %get-tuple-element.114), channel_id=1, source_target_pairs={{0,6},{1,7},{2,4},{3,5},{4,2},{5,3},{6,0},{7,1},{8,14},{9,15},{10,... | collective-permute-start | bytes 196616 | tf_op jit(solution)/shard_map/ppermute | solution.py:772
  383.8 5.2 %collective-permute-start.22 = (bf16[32,1024]{1,0:T(8,128)(2,1)S(1)}, bf16[32,1024]{1,0:T(8,128)(2,1)S(1)}, u32[]{:S(2)}, u32[]{:S(2)}) collective-permute-start(bf16[32,1024]{1,0:T(8,128)(2,1)S(1)} %get-tuple-element.115), channel_id=1, source_target_pairs={{0,4},{1,5},{2,6},{3,7},{4,0},{5,1},{6,2},{7,3},{8,12},{9,13},{10,... | collective-permute-start | bytes 196616 | tf_op jit(solution)/shard_map/ppermute | solution.py:772
  386.1 20.5 %collective-permute-start.9 = (bf16[4,2,32,1536]{3,2,0,1:T(8,128)(2,1)S(1)}, bf16[4,2,32,1536]{3,2,0,1:T(8,128)(2,1)S(1)}, u32[]{:S(2)}, u32[]{:S(2)}) collective-permute-start(bf16[4,2,32,1536]{3,2,0,1:T(8,128)(2,1)S(1)} %bitcast.269), channel_id=1, source_target_pairs={{0,16},{1,17},{2,18},{3,19},{4,20},{5,21},{6,22},{7,23},{8,24},{9,... | collective-permute-start | bytes 2359304 | tf_op jit(solution)/shard_map/ppermute | solution.py:772
  395.0 13.4 %copy-start.5 = (bf16[512,4096]{1,0:T(8,128)(2,1)S(1)}, bf16[512,4096]{1,0:T(8,128)(2,1)}, u32[]{:S(2)}) copy-start(bf16[512,4096]{1,0:T(8,128)(2,1)} %convolution_convert_fusion) | copy-start | bytes 12582916
  395.3 21.6 %collective-permute-start.12 = (bf16[4,32,1536]{2,1,0:T(8,128)(2,1)S(1)}, bf16[4,32,1536]{2,1,0:T(8,128)(2,1)S(1)}, u32[]{:S(2)}, u32[]{:S(2)}) collective-permute-start(bf16[4,32,1536]{2,1,0:T(8,128)(2,1)S(1)} %dynamic-slice_bitcast_fusion.10), channel_id=1, source_target_pairs={{0,16},{1,17},{2,18},{3,19},{4,20},{5,21},{6,22},{7,23},{8,24},{9,... | collective-permute-start | bytes 1179656 | tf_op jit(solution)/shard_map/ppermute | solution.py:772
  407.6 12.4 %collective-permute-start.10 = (bf16[4,32,1536]{2,1,0:T(8,128)(2,1)}, bf16[4,32,1536]{2,1,0:T(8,128)(2,1)}, u32[]{:S(2)}, u32[]{:S(2)}) collective-permute-start(bf16[4,32,1536]{2,1,0:T(8,128)(2,1)} %dynamic-slice_bitcast_fusion.11), channel_id=1, source_target_pairs={{0,1},{1,0},{2,3},{3,2},{4,5},{5,4},{6,7},{7,6},{8,9},{9,8},{10,11... | collective-permute-start | bytes 1179656 | tf_op jit(solution)/shard_map/ppermute | solution.py:772
  410.8 3.2 copy-start.4
  411.1 31.3 %collective-permute-start.27 = (bf16[2,4,32,2048]{3,2,1,0:T(8,128)(2,1)S(1)}, bf16[2,4,32,2048]{3,2,1,0:T(8,128)(2,1)S(1)}, u32[]{:S(2)}, u32[]{:S(2)}) collective-permute-start(bf16[2,4,32,2048]{3,2,1,0:T(8,128)(2,1)S(1)} %dynamic-slice_bitcast_fusion.1), channel_id=1, source_target_pairs={{0,1},{1,0},{2,3},{3,2},{4,5},{5,4},{6,7},{7,6},{8,9},{9,8},{10,11... | collective-permute-start | bytes 3145736 | tf_op jit(solution)/shard_map/ppermute | solution.py:772
  412.3 32.3 %collective-permute-start.25 = (bf16[4,2,32,2048]{3,2,0,1:T(8,128)(2,1)S(1)}, bf16[4,2,32,2048]{3,2,0,1:T(8,128)(2,1)S(1)}, u32[]{:S(2)}, u32[]{:S(2)}) collective-permute-start(bf16[4,2,32,2048]{3,2,0,1:T(8,128)(2,1)S(1)} %bitcast.267), channel_id=1, source_target_pairs={{0,16},{1,17},{2,18},{3,19},{4,20},{5,21},{6,22},{7,23},{8,24},{9,... | collective-permute-start | bytes 3145736 | tf_op jit(solution)/shard_map/ppermute | solution.py:772
  421.2 5.7 %collective-permute-start.13 = (bf16[32,3072]{1,0:T(8,128)(2,1)S(1)}, bf16[32,3072]{1,0:T(8,128)(2,1)S(1)}, u32[]{:S(2)}, u32[]{:S(2)}) collective-permute-start(bf16[32,3072]{1,0:T(8,128)(2,1)S(1)} %get-tuple-element.108), channel_id=1, source_target_pairs={{0,2},{1,3},{2,0},{3,1},{4,6},{5,7},{6,4},{7,5},{8,10},{9,11},{10,... | collective-permute-start | bytes 589832 | tf_op jit(solution)/shard_map/ppermute | solution.py:772
  422.4 8.5 %collective-permute-start.15 = (bf16[32,3072]{1,0:T(8,128)(2,1)S(1)}, bf16[32,3072]{1,0:T(8,128)(2,1)S(1)}, u32[]{:S(2)}, u32[]{:S(2)}) collective-permute-start(bf16[32,3072]{1,0:T(8,128)(2,1)S(1)} %get-tuple-element.109), channel_id=1, source_target_pairs={{0,6},{1,7},{2,4},{3,5},{4,2},{5,3},{6,0},{7,1},{8,14},{9,15},{10,... | collective-permute-start | bytes 589832 | tf_op jit(solution)/shard_map/ppermute | solution.py:772
  425.1 10.5 %collective-permute-start.14 = (bf16[32,3072]{1,0:T(8,128)(2,1)S(1)}, bf16[32,3072]{1,0:T(8,128)(2,1)S(1)}, u32[]{:S(2)}, u32[]{:S(2)}) collective-permute-start(bf16[32,3072]{1,0:T(8,128)(2,1)S(1)} %get-tuple-element.110), channel_id=1, source_target_pairs={{0,4},{1,5},{2,6},{3,7},{4,0},{5,1},{6,2},{7,3},{8,12},{9,13},{10,... | collective-permute-start | bytes 589832 | tf_op jit(solution)/shard_map/ppermute | solution.py:772
  426.9 37.8 %collective-permute-start.35 = (bf16[2,4,128,512]{3,2,1,0:T(8,128)(2,1)S(1)}, bf16[2,4,128,512]{3,2,1,0:T(8,128)(2,1)S(1)}, u32[]{:S(2)}, u32[]{:S(2)}) collective-permute-start(bf16[2,4,128,512]{3,2,1,0:T(8,128)(2,1)S(1)} %dynamic-slice_bitcast_fusion), channel_id=1, source_target_pairs={{0,1},{1,0},{2,3},{3,2},{4,5},{5,4},{6,7},{7,6},{8,9},{9,8},{10,11... | collective-permute-start | bytes 3145736 | tf_op jit(solution)/shard_map/ppermute | solution.py:772
  430.9 36.1 %collective-permute-start.33 = (bf16[4,2,128,512]{3,2,0,1:T(8,128)(2,1)S(1)}, bf16[4,2,128,512]{3,2,0,1:T(8,128)(2,1)S(1)}, u32[]{:S(2)}, u32[]{:S(2)}) collective-permute-start(bf16[4,2,128,512]{3,2,0,1:T(8,128)(2,1)S(1)} %bitcast.268), channel_id=1, source_target_pairs={{0,16},{1,17},{2,18},{3,19},{4,20},{5,21},{6,22},{7,23},{8,24},{9,... | collective-permute-start | bytes 3145736 | tf_op jit(solution)/shard_map/ppermute | solution.py:772
  442.8 29.3 %collective-permute-start.28 = (bf16[4,32,2048]{2,1,0:T(8,128)(2,1)S(1)}, bf16[4,32,2048]{2,1,0:T(8,128)(2,1)S(1)}, u32[]{:S(2)}, u32[]{:S(2)}) collective-permute-start(bf16[4,32,2048]{2,1,0:T(8,128)(2,1)S(1)} %dynamic-slice_bitcast_fusion.8), channel_id=1, source_target_pairs={{0,16},{1,17},{2,18},{3,19},{4,20},{5,21},{6,22},{7,23},{8,24},{9,... | collective-permute-start | bytes 1572872 | tf_op jit(solution)/shard_map/ppermute | solution.py:772
  445.0 27.4 %collective-permute-start.26 = (bf16[4,32,2048]{2,1,0:T(8,128)(2,1)S(1)}, bf16[4,32,2048]{2,1,0:T(8,128)(2,1)S(1)}, u32[]{:S(2)}, u32[]{:S(2)}) collective-permute-start(bf16[4,32,2048]{2,1,0:T(8,128)(2,1)S(1)} %dynamic-slice_bitcast_fusion.9), channel_id=1, source_target_pairs={{0,1},{1,0},{2,3},{3,2},{4,5},{5,4},{6,7},{7,6},{8,9},{9,8},{10,11... | collective-permute-start | bytes 1572872 | tf_op jit(solution)/shard_map/ppermute | solution.py:772
  465.2 13.1 %collective-permute-start.36 = (bf16[4,128,512]{2,1,0:T(8,128)(2,1)S(1)}, bf16[4,128,512]{2,1,0:T(8,128)(2,1)S(1)}, u32[]{:S(2)}, u32[]{:S(2)}) collective-permute-start(bf16[4,128,512]{2,1,0:T(8,128)(2,1)S(1)} %dynamic-slice_bitcast_fusion.6), channel_id=1, source_target_pairs={{0,16},{1,17},{2,18},{3,19},{4,20},{5,21},{6,22},{7,23},{8,24},{9,... | collective-permute-start | bytes 1572872 | tf_op jit(solution)/shard_map/ppermute | solution.py:772
  467.4 11.1 %collective-permute-start.34 = (bf16[4,128,512]{2,1,0:T(8,128)(2,1)S(1)}, bf16[4,128,512]{2,1,0:T(8,128)(2,1)S(1)}, u32[]{:S(2)}, u32[]{:S(2)}) collective-permute-start(bf16[4,128,512]{2,1,0:T(8,128)(2,1)S(1)} %dynamic-slice_bitcast_fusion.7), channel_id=1, source_target_pairs={{0,1},{1,0},{2,3},{3,2},{4,5},{5,4},{6,7},{7,6},{8,9},{9,8},{10,11... | collective-permute-start | bytes 1572872 | tf_op jit(solution)/shard_map/ppermute | solution.py:772
  472.8 16.8 %collective-permute-start.29 = (bf16[32,4096]{1,0:T(8,128)(2,1)S(1)}, bf16[32,4096]{1,0:T(8,128)(2,1)S(1)}, u32[]{:S(2)}, u32[]{:S(2)}) collective-permute-start(bf16[32,4096]{1,0:T(8,128)(2,1)S(1)} %get-tuple-element.103), channel_id=1, source_target_pairs={{0,2},{1,3},{2,0},{3,1},{4,6},{5,7},{6,4},{7,5},{8,10},{9,11},{10,... | collective-permute-start | bytes 786440 | tf_op jit(solution)/shard_map/ppermute | solution.py:772
  472.9 17.4 %collective-permute-start.31 = (bf16[32,4096]{1,0:T(8,128)(2,1)S(1)}, bf16[32,4096]{1,0:T(8,128)(2,1)S(1)}, u32[]{:S(2)}, u32[]{:S(2)}) collective-permute-start(bf16[32,4096]{1,0:T(8,128)(2,1)S(1)} %get-tuple-element.104), channel_id=1, source_target_pairs={{0,6},{1,7},{2,4},{3,5},{4,2},{5,3},{6,0},{7,1},{8,14},{9,15},{10,... | collective-permute-start | bytes 786440 | tf_op jit(solution)/shard_map/ppermute | solution.py:772
  476.5 30.0 %collective-permute-start.30 = (bf16[32,4096]{1,0:T(8,128)(2,1)S(1)}, bf16[32,4096]{1,0:T(8,128)(2,1)S(1)}, u32[]{:S(2)}, u32[]{:S(2)}) collective-permute-start(bf16[32,4096]{1,0:T(8,128)(2,1)S(1)} %get-tuple-element.105), channel_id=1, source_target_pairs={{0,4},{1,5},{2,6},{3,7},{4,0},{5,1},{6,2},{7,3},{8,12},{9,13},{10,... | collective-permute-start | bytes 786440 | tf_op jit(solution)/shard_map/ppermute | solution.py:772
  478.9 28.6 %collective-permute-start.37 = (bf16[128,1024]{1,0:T(8,128)(2,1)S(1)}, bf16[128,1024]{1,0:T(8,128)(2,1)S(1)}, u32[]{:S(2)}, u32[]{:S(2)}) collective-permute-start(bf16[128,1024]{1,0:T(8,128)(2,1)S(1)} %get-tuple-element.100), channel_id=1, source_target_pairs={{0,2},{1,3},{2,0},{3,1},{4,6},{5,7},{6,4},{7,5},{8,10},{9,11},{10,... | collective-permute-start | bytes 786440 | tf_op jit(solution)/shard_map/ppermute | solution.py:772
  479.0 28.5 %collective-permute-start.39 = (bf16[128,1024]{1,0:T(8,128)(2,1)S(1)}, bf16[128,1024]{1,0:T(8,128)(2,1)S(1)}, u32[]{:S(2)}, u32[]{:S(2)}) collective-permute-start(bf16[128,1024]{1,0:T(8,128)(2,1)S(1)} %get-tuple-element.101), channel_id=1, source_target_pairs={{0,6},{1,7},{2,4},{3,5},{4,2},{5,3},{6,0},{7,1},{8,14},{9,15},{10,... | collective-permute-start | bytes 786440 | tf_op jit(solution)/shard_map/ppermute | solution.py:772
  489.6 22.6 %collective-permute-start.38 = (bf16[128,1024]{1,0:T(8,128)(2,1)S(1)}, bf16[128,1024]{1,0:T(8,128)(2,1)S(1)}, u32[]{:S(2)}, u32[]{:S(2)}) collective-permute-start(bf16[128,1024]{1,0:T(8,128)(2,1)S(1)} %get-tuple-element.102), channel_id=1, source_target_pairs={{0,4},{1,5},{2,6},{3,7},{4,0},{5,1},{6,2},{7,3},{8,12},{9,13},{10,... | collective-permute-start | bytes 786440 | tf_op jit(solution)/shard_map/ppermute | solution.py:772
